TPU v7x, 32 devices: a whole 2x2x4 slice. The times are simulated.
32 devices in a mesh: rel: 4 (over y, x), ent: 8 (over z, core).
Axes of the slice: x: 2, y: 2, z: 4, core: 2. Of those that a mesh axis runs over, the one named last changes fastest.
Arguments:
- ent_table: float32 [16384, 400], P('ent'), may hold values from -0.3 to 0.3
- entity_first_moment: float32 [16384, 400], P('ent'), may hold values from -2.037372e-09 to 2.037372e-09
- ent_v: float32 [16384, 400], P('ent'), may hold values from 2.144052e-20 to 8.576208e-20
- rel_table: float32 [3, 6400, 400], P(None, ('rel', 'ent')), may hold values from -0.3 to 0.3
- relation_first_moment: float32 [3, 6400, 400], P(None, ('rel', 'ent')), may hold values from -2.037372e-09 to 2.037372e-09
- rel_v: float32 [3, 6400, 400], P(None, ('rel', 'ent')), may hold values from 2.144052e-20 to 8.576208e-20
- src_ids: int32 [4, 8, 8, 1280], P('rel', 'ent'), may hold values from 0 to 2047
- rel_ids: int32 [4, 8, 8, 1280], P('rel', 'ent'), may hold values from 0 to 1599
- dst_ids: int32 [4, 8, 8, 1280], P('rel', 'ent'), may hold values from 0 to 2047
- neg_ids: int32 [4, 8, 8, 1000], P('rel', 'ent'), may hold values from 0 to 2047
- bucket_counts: int32 [4, 8, 8], P('rel', 'ent'), may hold values from 256 to 1280, as said below
Outputs:
- loss_sum: float32 [], replicated
- edge_count: float32 [], replicated
- grad_norm: float32 [], replicated
- new_ent: float32 [16384, 400], P('ent')
- new_ent_m: float32 [16384, 400], P('ent')
- new_ent_v: float32 [16384, 400], P('ent')
- ent_copy: bfloat16 [16384, 400], P('ent')
- new_rel: float32 [3, 6400, 400], P(None, ('rel', 'ent'))
- new_rel_m: float32 [3, 6400, 400], P(None, ('rel', 'ent'))
- new_rel_v: float32 [3, 6400, 400], P(None, ('rel', 'ent'))
- rel_copy: bfloat16 [3, 6400, 400], P(None, ('rel', 'ent'))
Inputs may be any that keep to these rules, and one draw needn't show every extreme that they name: `bucket_counts`: each sender's row of 8 buckets holds one bucket filled to 1280.
All inputs are finite; a program needn't handle non-finite values.
Results may differ from a plain program's by a relative error of at most 0.0034.
Values may be sent and summed in bfloat16 or wider, within the bound.
A program may use at most 512 MiB of HBM per device.

v0:
```python
import math

import jax
import jax.numpy as jnp
from jax import lax
from jax.sharding import PartitionSpec as P

STEP = 10


margin = 2.5
beta_one = 0.9
beta_two = 0.999
learn_rate = 0.05
decay_rate = 0.01
epsilon = 1e-16


def shortened(array):
    return jax.tree.map(lambda a: a.astype(jnp.bfloat16) if a.dtype == jnp.float32 else a, array)


def adamw(weight, moment, second, grad):
    moment = beta_one * moment + (1.0 - beta_one) * grad
    second = beta_two * second + (1.0 - beta_two) * grad * grad
    m_hat = moment / (1.0 - beta_one**STEP)
    v_hat = second / (1.0 - beta_two**STEP)
    weight = weight - learn_rate * (m_hat / (jnp.sqrt(v_hat) + epsilon) + decay_rate * weight)
    return (weight, moment, second)


def body(
    ent_table,
    entity_first_moment,
    ent_v,
    rel_table,
    relation_first_moment,
    rel_v,
    src_ids,
    rel_ids,
    dst_ids,
    neg_ids,
    bucket_counts,
):
    parts = src_ids.shape[2]
    slots = src_ids.shape[3]
    width = ent_table.shape[1]
    negcount = neg_ids.shape[3]
    clip_level = 0.01 / math.sqrt(lax.axis_size("rel") * lax.axis_size("ent") * parts * slots)
    ent_low = ent_table.astype(jnp.bfloat16)
    layers = lax.all_gather(rel_table.astype(jnp.bfloat16), "ent", axis=1, tiled=True)
    rel_sum = (
        layers[0].astype(jnp.float32)
        + layers[1].astype(jnp.float32)
        + layers[2].astype(jnp.float32)
    )
    sources = src_ids[0, 0]
    relation = rel_ids[0, 0]
    counts = bucket_counts[0, 0]
    hidden = ent_low[sources].astype(jnp.float32) + rel_sum[relation]
    total = lax.psum(jnp.sum(counts).astype(jnp.float32), ("rel", "ent"))
    arrived, dst_in, count_in = (
        lax.all_to_all(hidden.astype(jnp.bfloat16), "ent", split_axis=0, concat_axis=0, tiled=True),
        lax.all_to_all(dst_ids[0, 0], "ent", split_axis=0, concat_axis=0, tiled=True),
        lax.all_to_all(counts[:, None], "ent", split_axis=0, concat_axis=0, tiled=True),
    )
    live = (jnp.arange(slots, dtype=jnp.int32)[None, :] < count_in).astype(jnp.float32)
    negatives = neg_ids[0, 0]

    def block(args):
        hid, dst, neg, alive = args
        weight = alive / total
        hid_f = hid.astype(jnp.float32)
        diff = hid_f - ent_low[dst].astype(jnp.float32)
        pos_dist = jnp.sqrt(jnp.sum(diff * diff, -1) + 1.0)
        rows = ent_low[neg]
        rows_f = rows.astype(jnp.float32)
        prod = lax.dot_general(
            hid, rows, (((1,), (1,)), ((), ())), preferred_element_type=jnp.float32
        )
        sq = (
            jnp.sum(hid_f * hid_f, -1)[:, None] + jnp.sum(rows_f * rows_f, -1)[None, :] - 2.0 * prod
        )
        neg_dist = jnp.sqrt(sq + 1.0)
        per_edge = jax.nn.softplus(pos_dist - margin) + jnp.mean(
            jax.nn.softplus(margin - neg_dist), -1
        )
        loss = jnp.sum(alive * per_edge)
        g_pos = weight * jax.nn.sigmoid(pos_dist - margin)
        g_diff = (g_pos / pos_dist)[:, None] * diff
        g_sq = -(weight[:, None] / negcount) * jax.nn.sigmoid(margin - neg_dist) / (2.0 * neg_dist)
        g_prod = (-2.0 * g_sq).astype(jnp.bfloat16)
        g_hid = (
            g_diff
            + 2.0 * hid_f * jnp.sum(g_sq, 1)[:, None]
            + jnp.dot(g_prod, rows, preferred_element_type=jnp.float32)
        )
        g_rows = 2.0 * rows_f * jnp.sum(g_sq, 0)[:, None] + lax.dot_general(
            g_prod, hid, (((0,), (0,)), ((), ())), preferred_element_type=jnp.float32
        )
        return (loss, g_hid.astype(jnp.bfloat16), -g_diff, g_rows)

    losses, back, g_target, g_negative = lax.map(
        block, (arrived, dst_in, negatives, live), batch_size=min(4, parts)
    )
    returned = (
        jax.tree.map(
            lambda part, own: part.astype(own.dtype),
            lax.all_to_all(shortened(back), "ent", split_axis=0, concat_axis=0, tiled=True),
            back,
        )
        .reshape(-1, width)
        .astype(jnp.float32)
    )
    ent_grad = jnp.zeros(ent_table.shape, jnp.float32)
    ent_grad = ent_grad.at[dst_in.reshape(-1)].add(g_target.reshape(-1, width))
    ent_grad = ent_grad.at[negatives.reshape(-1)].add(g_negative.reshape(-1, width))
    ent_grad = ent_grad.at[sources.reshape(-1)].add(returned)
    ent_grad = lax.psum(ent_grad, "rel")
    rel_local = jnp.zeros(rel_sum.shape, jnp.float32).at[relation.reshape(-1)].add(returned)
    rel_grad = lax.psum_scatter(rel_local, "ent", scatter_dimension=0, tiled=True)
    own_squares = jnp.where(
        lax.axis_index("rel") == 0, jnp.sum(ent_grad * ent_grad), 0.0
    ) + 3.0 * jnp.sum(rel_grad * rel_grad)
    squares, loss_sum = lax.psum((own_squares, jnp.sum(losses)), ("rel", "ent"))
    grad_norm = jnp.sqrt(squares)
    scale = jnp.minimum(1.0, clip_level / grad_norm)
    new_ent, new_ent_m, new_ent_v = adamw(ent_table, entity_first_moment, ent_v, scale * ent_grad)
    new_rel, new_rel_m, new_rel_v = adamw(
        rel_table, relation_first_moment, rel_v, scale * rel_grad[None]
    )
    return (
        loss_sum,
        total,
        grad_norm,
        new_ent,
        new_ent_m,
        new_ent_v,
        new_ent.astype(jnp.bfloat16),
        new_rel,
        new_rel_m,
        new_rel_v,
        new_rel.astype(jnp.bfloat16),
    )


def solution(mesh):
    return jax.shard_map(
        body,
        mesh=mesh,
        in_specs=(
            P("ent", None),
            P("ent", None),
            P("ent", None),
            P(None, ("rel", "ent"), None),
            P(None, ("rel", "ent"), None),
            P(None, ("rel", "ent"), None),
            P("rel", "ent", None, None),
            P("rel", "ent", None, None),
            P("rel", "ent", None, None),
            P("rel", "ent", None, None),
            P("rel", "ent", None),
        ),
        out_specs=(
            P(),
            P(),
            P(),
            P("ent", None),
            P("ent", None),
            P("ent", None),
            P("ent", None),
            P(None, ("rel", "ent"), None),
            P(None, ("rel", "ent"), None),
            P(None, ("rel", "ent"), None),
            P(None, ("rel", "ent"), None),
        ),
        check_vma=False,
    )
```

profile of v0, /device:TPU:8, one launch (start us, length us, event | category | flops | bytes accessed | tf_op | source)
XLA Modules:
  0.0 1149.0 jit_solution(10167225701056576695)
XLA Ops:
  7.2 2.2 convert_element_type.97
  9.4 1.3 copy.121
  10.8 5.3 all-to-all-start
  16.1 1.4 all_to_all.21
  17.5 0.8 compare_select_fusion.9
  18.3 0.8 compare_select_fusion.8
  19.1 3.2 copy.122
  22.4 41.7 %gather_fusion.2 = bf16[10240,400]{1,0:T(8,128)(2,1)} fusion(bf16[2048,400]{1,0:T(8,128)(2,1)S(1)} %copy.122, s32[10240]{0:T(1024)S(1)} %broadcast_clamp_fusion.2), kind=kCustom, calls=%fused_computation.2 | custom fusion | bytes 16424960 | tf_op jit(solution)/shard_map/gather | solution.py:60
  64.1 4.8 add_bitcast_fusion
  68.9 45.4 %gather_fusion.3 = f32[10240,400]{1,0:T(8,128)} fusion(f32[1600,400]{1,0:T(8,128)} %add_bitcast_fusion, s32[10240]{0:T(1024)S(1)} %broadcast_clamp_fusion.1), kind=kCustom, calls=%fused_computation.3 | custom fusion | bytes 32808960 | tf_op jit(solution)/shard_map/gather | solution.py:60
  114.3 5.1 all-to-all-start.2
  119.4 15.6 %add_convert_fusion = bf16[10240,400]{1,0:T(8,128)(2,1)} fusion(f32[10240,400]{1,0:T(8,128)} %gather_fusion.3, bf16[10240,400]{1,0:T(8,128)(2,1)} %gather_fusion.2), kind=kLoop, calls=%fused_computation.55 | loop fusion | flops 12288000 | bytes 32768000 | tf_op jit(solution)/shard_map/convert_element_type | solution.py:63
  134.9 13.9 %copy.123 = bf16[8,1280,400]{1,2,0:T(8,128)(2,1)} copy(bf16[8,1280,400]{2,1,0:T(8,128)(2,1)} %bitcast.116) | data formatting | bytes 16384000 | tf_op jit(solution)/shard_map/convert_element_type | solution.py:63
  148.8 5.2 all-to-all-start.1
  154.1 0.6 reduce_sum.120
  155.3 196.6 %psum.28 = f32[]{:T(128)} all-reduce(f32[]{:T(128)S(6)} %convert_element_type.102), channel_id=1, replica_groups=mesh['rel'=4,'ent'=8] {'rel','ent'}, use_global_device_ids=true, to_apply=%region_1.0 | all-reduce | flops 1 | bytes 8 | tf_op jit(solution)/shard_map/psum | solution.py:61
  352.5 329.5 %while.18 = (s32[]{:T(128)}, f32[2,4]{1,0:T(2,128)S(1)}, bf16[2,4,1280,400]{2,3,1,0:T(8,128)(2,1)}, f32[2,4,1280,400]{2,3,1,0:T(8,128)}, f32[2,4,1000,400]{2,3,1...) while((s32[]{:T(128)}, f32[2,4]{1,0:T(2,128)S(1)}, ...), condition=%wide.region_10.11_spmd, body=%wide.region_2.10_spmd.sunk | while | flops 12457467904 | bytes 206755568 | solution.py:103
  366.0 0.7 multiply_negate_fusion.2
  366.7 17.2 %gather_fusion.1 = bf16[4000,400]{1,0:T(8,128)(2,1)} fusion(bf16[2048,400]{1,0:T(8,128)(2,1)S(1)} %get-tuple-element.361, s32[4096]{0:T(1024)S(1)} %pad_clamp_fusion.2), kind=kCustom, calls=%fused_computation.1.clone.1 | custom fusion | bytes 6416000 | tf_op jit(solution)/shard_map/while/body/eval_jaxpr/vmap()/gather | solution.py:76
  383.9 6.0 copy.147
  389.9 2.7 fusion.47
  392.6 21.4 %gather_fusion = bf16[5120,400]{1,0:T(8,128)(2,1)} fusion(bf16[2048,400]{1,0:T(8,128)(2,1)S(1)} %get-tuple-element.361, s32[5120]{0:T(1024)S(1)} %broadcast_clamp_fusion.4), kind=kCustom, calls=%fused_computation.clone.1 | custom fusion | bytes 8212480 | tf_op jit(solution)/shard_map/while/body/eval_jaxpr/vmap()/gather | solution.py:74
  414.0 7.9 convert_element_type.175
  421.8 10.6 copy.146
  432.4 6.3 multiply_reduce_fusion.4
  438.7 10.4 copy.148
  449.1 36.0 %fusion.48 = (f32[4,1000]{1,0:T(4,128)S(1)}, f32[4,1280]{1,0:T(4,128)S(1)}, f32[4,1280,1000]{1,2,0:T(8,128)}, f32[4,1280]{1,0:T(4,128)S(1)}) fusion(f32[4,1280]{1,0:T(4,128)S(1)} %multiply_negate_fusion.2, bf16[4,1000,400]{2,1,0:T(8,128)(2,1)} %bitcast.111, bf16[2,4,1280,400]{2,3,1,0:T(8,128)(2,1)} %get-tuple-element.359, s32[]{:T(128)S(6)} %copy.158, ...), kind=kOutput, calls=%fused_computation.83.clone.1 | convolution fusion | flops 4198385664 | bytes 28785924 | tf_op jit(solution)/shard_map/while/body/eval_jaxpr/vmap()/dot_general | solution.py:78
  485.1 0.8 fusion.49
  486.0 16.2 %bitcast_dynamic-update-slice_fusion.2 = bf16[2,4,1280,400]{2,3,1,0:T(8,128)(2,1)} fusion(bf16[2,4,1280,400]{2,3,1,0:T(8,128)(2,1)} %get-tuple-element.342, s32[]{:T(128)S(6)} %copy.158, bf16[4,1000,400]{2,1,0:T(8,128)(2,1)} %bitcast.112, f32[4,1280,1000]{1,2,0:T(8,128)} %get-tuple-element.323, f32[4,1280]{1,0:T(4,128)S(1)} %get-tuple-element.324, ...), kind=kOutput, calls=%fused_computation.29.clone.1 | convolution fusion | flops 4120576000 | bytes 41000964 | tf_op jit(solution)/shard_map/while/body/eval_jaxpr/vmap()/dot_general | solution.py:96
  502.2 13.0 %fusion.50 = f32[2,4,1000,400]{2,3,1,0:T(8,128)} fusion(f32[2,4,1000,400]{2,3,1,0:T(8,128)} %get-tuple-element.344, s32[]{:T(128)S(6)} %copy.158, bf16[4,1000,400]{1,2,0:T(8,128)(2,1)} %copy.147, f32[4,1000]{1,0:T(4,128)S(1)} %broadcast_multiply_fusion.3, f32[4,1280,1000]{1,2,0:T(8,128)} %get-tuple-element.323, ...), kind=kOutput, calls=%fused_computation.28.clone.1 | convolution fusion | flops 4111040000 | bytes 34423424 | tf_op jit(solution)/shard_map/while/body/eval_jaxpr/vmap()/dot_general | solution.py:98
  515.2 8.7 negate_dynamic-update-slice_fusion.2
  524.1 0.7 multiply_negate_fusion.2
  524.8 17.2 %gather_fusion.1 = bf16[4000,400]{1,0:T(8,128)(2,1)} fusion(bf16[2048,400]{1,0:T(8,128)(2,1)S(1)} %get-tuple-element.361, s32[4096]{0:T(1024)S(1)} %pad_clamp_fusion.2), kind=kCustom, calls=%fused_computation.1.clone.1 | custom fusion | bytes 6416000 | tf_op jit(solution)/shard_map/while/body/eval_jaxpr/vmap()/gather | solution.py:76
  542.0 6.0 copy.147
  548.0 2.7 fusion.47
  550.7 21.4 %gather_fusion = bf16[5120,400]{1,0:T(8,128)(2,1)} fusion(bf16[2048,400]{1,0:T(8,128)(2,1)S(1)} %get-tuple-element.361, s32[5120]{0:T(1024)S(1)} %broadcast_clamp_fusion.4), kind=kCustom, calls=%fused_computation.clone.1 | custom fusion | bytes 8212480 | tf_op jit(solution)/shard_map/while/body/eval_jaxpr/vmap()/gather | solution.py:74
  572.1 7.9 convert_element_type.175
  579.9 10.6 copy.146
  590.5 6.2 multiply_reduce_fusion.4
  596.7 10.4 copy.148
  607.2 36.0 %fusion.48 = (f32[4,1000]{1,0:T(4,128)S(1)}, f32[4,1280]{1,0:T(4,128)S(1)}, f32[4,1280,1000]{1,2,0:T(8,128)}, f32[4,1280]{1,0:T(4,128)S(1)}) fusion(f32[4,1280]{1,0:T(4,128)S(1)} %multiply_negate_fusion.2, bf16[4,1000,400]{2,1,0:T(8,128)(2,1)} %bitcast.111, bf16[2,4,1280,400]{2,3,1,0:T(8,128)(2,1)} %get-tuple-element.359, s32[]{:T(128)S(6)} %copy.158, ...), kind=kOutput, calls=%fused_computation.83.clone.1 | convolution fusion | flops 4198385664 | bytes 28785924 | tf_op jit(solution)/shard_map/while/body/eval_jaxpr/vmap()/dot_general | solution.py:78
  643.2 0.8 fusion.49
  644.0 16.2 %bitcast_dynamic-update-slice_fusion.2 = bf16[2,4,1280,400]{2,3,1,0:T(8,128)(2,1)} fusion(bf16[2,4,1280,400]{2,3,1,0:T(8,128)(2,1)} %get-tuple-element.342, s32[]{:T(128)S(6)} %copy.158, bf16[4,1000,400]{2,1,0:T(8,128)(2,1)} %bitcast.112, f32[4,1280,1000]{1,2,0:T(8,128)} %get-tuple-element.323, f32[4,1280]{1,0:T(4,128)S(1)} %get-tuple-element.324, ...), kind=kOutput, calls=%fused_computation.29.clone.1 | convolution fusion | flops 4120576000 | bytes 41000964 | tf_op jit(solution)/shard_map/while/body/eval_jaxpr/vmap()/dot_general | solution.py:96
  660.3 13.0 %fusion.50 = f32[2,4,1000,400]{2,3,1,0:T(8,128)} fusion(f32[2,4,1000,400]{2,3,1,0:T(8,128)} %get-tuple-element.344, s32[]{:T(128)S(6)} %copy.158, bf16[4,1000,400]{1,2,0:T(8,128)(2,1)} %copy.147, f32[4,1000]{1,0:T(4,128)S(1)} %broadcast_multiply_fusion.3, f32[4,1280,1000]{1,2,0:T(8,128)} %get-tuple-element.323, ...), kind=kOutput, calls=%fused_computation.28.clone.1 | convolution fusion | flops 4111040000 | bytes 34423424 | tf_op jit(solution)/shard_map/while/body/eval_jaxpr/vmap()/dot_general | solution.py:98
  673.3 8.7 negate_dynamic-update-slice_fusion.2
  682.6 7.0 all-to-all-start.3
  689.9 15.1 %copy.137 = f32[2,4,1000,400]{3,2,1,0:T(8,128)} copy(f32[2,4,1000,400]{2,3,1,0:T(8,128)} %get-tuple-element.153) | data formatting | bytes 25600000 | tf_op jit(solution)/shard_map/reshape;reshape | solution.py:117
  705.1 20.1 %copy.136 = f32[2,4,1280,400]{3,2,1,0:T(8,128)} copy(f32[2,4,1280,400]{2,3,1,0:T(8,128)} %get-tuple-element.152) | data formatting | bytes 32768000 | tf_op jit(solution)/shard_map/reshape;reshape | solution.py:116
  725.2 63.3 %scatter_custom_fusion = f32[2048,400]{1,0:T(8,128)} fusion(s32[10240]{0:T(1024)S(1)} %bitcast.124, f32[10240,400]{1,0:T(8,128)} %bitcast.117, f32[]{:T(128)} %constant.71.clone.1), kind=kCustom, calls=%fused_computation.62 | custom fusion | flops 4096000 | bytes 3277312 | tf_op jit(solution)/shard_map/scatter-add | solution.py:116
  788.4 53.3 %scatter_fusion = f32[2048,400]{1,0:T(8,128)} fusion(f32[2048,400]{1,0:T(8,128)} %scatter_custom_fusion, s32[8000]{0:T(1024)S(1)} %fusion.30, f32[8000,400]{1,0:T(8,128)} %bitcast.115), kind=kCustom, calls=%fused_computation.5 | custom fusion | flops 3200000 | bytes 38432000 | tf_op jit(solution)/shard_map/scatter-add | solution.py:117
  841.8 23.9 %all-to-all-done.3 = bf16[8,1280,400]{1,2,0:T(8,128)(2,1)} async-done(((bf16[8,1280,400]{1,2,0:T(8,128)(2,1)}), bf16[8,1280,400]{1,2,0:T(8,128)(2,1)}, u32[]{:S(2)}, u32[]{:S(2)}) %all-to-all-start.3) | async-done | bytes 8192032 | tf_op jit(solution)/shard_map/all_to_all | solution.py:109
  865.7 14.9 %copy.128 = f32[8,1280,400]{2,1,0:T(8,128)} copy(bf16[8,1280,400]{1,2,0:T(8,128)(2,1)} %all-to-all-done.3) | data formatting | bytes 24576000 | tf_op jit(solution)/shard_map/convert_element_type | solution.py:113
  880.7 65.2 %scatter_fusion.1 = f32[2048,400]{1,0:T(8,128)} fusion(f32[2048,400]{1,0:T(8,128)} %scatter_fusion, s32[10240]{0:T(1024)S(1)} %bitcast.120, f32[10240,400]{1,0:T(8,128)} %bitcast.113), kind=kCustom, calls=%fused_computation.6 | custom fusion | flops 4096000 | bytes 49192960 | tf_op jit(solution)/shard_map/scatter-add | solution.py:118
  945.8 5.2 copy.129
  951.2 63.1 %scatter_custom_fusion.3 = f32[1600,400]{1,0:T(8,128)} fusion(s32[10240]{0:T(1024)S(1)} %bitcast.125, f32[10240,400]{1,0:T(8,128)} %bitcast.114, f32[]{:T(128)} %constant.71.clone.1), kind=kCustom, calls=%fused_computation.64 | custom fusion | flops 4096000 | bytes 2560512 | tf_op jit(solution)/shard_map/scatter-add | solution.py:120
  1014.4 0.6 reduce_sum.121
  1015.0 27.6 %all-reduce.3.cloned.1.call-done = f32[2048,400]{0,1:T(8,128)} async-done(((f32[2048,400]{0,1:T(8,128)}), f32[2048,400]{0,1:T(8,128)}) %all-reduce.3.cloned.1.call-update) | async-done | bytes 3276816 | tf_op jit(solution)/shard_map/psum | solution.py:119
  1042.6 3.5 multiply_reduce_fusion.1
  1046.8 35.8 %reduce-scatter.2.cloned.1.call-done = f32[200,400]{1,0:T(8,128)} async-done(((f32[1600,400]{1,0:T(8,128)}), f32[200,400]{1,0:T(8,128)}) %reduce-scatter.2.cloned.1.call-update) | async-done | bytes 320016 | tf_op jit(solution)/shard_map/reduce_scatter | solution.py:121
  1082.6 1.7 multiply_reduce_fusion.2
  1085.0 43.7 %all-reduce = (f32[]{:T(128)}, f32[]{:T(128)}) all-reduce(f32[]{:T(128)} %reduce_sum.121, f32[]{:T(128)S(6)} %add.298), channel_id=1, replica_groups=mesh['rel'=4,'ent'=8] {'rel','ent'}, use_global_device_ids=true, to_apply=%region_12.13 | all-reduce | flops 2 | bytes 16 | tf_op jit(solution)/shard_map/psum | solution.py:125
  1129.4 1.3 multiply_multiply_fusion.1
  1130.7 5.2 fusion.32
  1136.0 5.2 fusion.33
  (73 shorter events, 2.1 us)
Async XLA Ops:
  7.2 56.9 %all-gather.2.cloned.1.call-start = ((), (), s32[]{:S(2)}) async-start(), calls=%async_computation.5 | async-start | bytes 5529600 | tf_op jit(solution)/shard_map/all_gather | solution.py:51
  10.8 103.5 %all-to-all-start = ((s32[8,1,1]{2,1,0:T(1,128)}), s32[8,1,1]{2,1,0:T(1,128)S(1)}, u32[]{:S(2)}, u32[]{:S(2)}) async-start(s32[8,1,1]{2,1,0:T(1,128)} %copy.121), calls=%async_computation | async-start | bytes 8192 | tf_op jit(solution)/shard_map/all_to_all | solution.py:65
  114.3 34.5 %all-to-all-start.2 = ((s32[8,1,1280]{2,1,0:T(1,128)}), s32[8,1,1280]{2,1,0:T(1,128)S(1)}, u32[]{:S(2)}, u32[]{:S(2)}) async-start(s32[8,1,1280]{2,1,0:T(1,128)} %all_to_all.21), calls=%async_computation.2 | async-start | bytes 81920 | tf_op jit(solution)/shard_map/all_to_all | solution.py:64
  148.8 5.3 copy-start.12
  148.8 203.2 %copy-start.8 = (s32[1,1,8,1000]{3,2,1,0:T(8,128)S(1)}, s32[1,1,8,1000]{3,2,1,0:T(8,128)}, u32[]{:S(2)}) copy-start(s32[1,1,8,1000]{3,2,1,0:T(8,128)} %param.22) | copy-start | bytes 96004
  148.8 203.6 %copy-start.4 = (s32[8,1,1280]{2,1,0:T(1,128)}, s32[8,1,1280]{2,1,0:T(1,128)S(1)}, u32[]{:S(2)}) copy-start(s32[8,1,1280]{2,1,0:T(1,128)S(1)} %all-to-all-done.2) | copy-start | bytes 122884
  148.8 203.7 %all-to-all-start.1 = ((bf16[8,1280,400]{1,2,0:T(8,128)(2,1)}), bf16[8,1280,400]{1,2,0:T(8,128)(2,1)}, u32[]{:S(2)}, u32[]{:S(2)}) async-start(bf16[8,1280,400]{1,2,0:T(8,128)(2,1)} %copy.123), calls=%async_computation.1 | async-start | bytes 16384000 | tf_op jit(solution)/shard_map/all_to_all | solution.py:63
  682.0 0.6 copy-start.10
  682.0 7.5 copy-start.9
  682.0 7.6 copy-start.6
  682.0 7.9 copy-start.5
  682.6 183.1 %all-to-all-start.3 = ((bf16[8,1280,400]{1,2,0:T(8,128)(2,1)}), bf16[8,1280,400]{1,2,0:T(8,128)(2,1)}, u32[]{:S(2)}, u32[]{:S(2)}) async-start(bf16[8,1280,400]{1,2,0:T(8,128)(2,1)} %bitcast.118), calls=%async_computation.3 | async-start | bytes 16384000 | tf_op jit(solution)/shard_map/all_to_all | solution.py:109
  689.5 353.1 %all-reduce.3.cloned.1.call-start = ((), (), s32[]{:S(2)}) async-start(), calls=%async_computation.6 | async-start | bytes 6553600 | tf_op jit(solution)/shard_map/psum | solution.py:119
  945.8 5.3 copy-start.7
  951.0 63.4 %copy-start.11 = (f32[2,4]{1,0:T(2,128)S(1)}, f32[2,4]{1,0:T(2,128)}, u32[]{:S(2)}) copy-start(f32[2,4]{1,0:T(2,128)} %copy-done.10) | copy-start | bytes 100
  951.1 131.5 %reduce-scatter.2.cloned.1.call-start = ((), (), s32[]{:S(2)}) async-start(), calls=%async_computation.7 | async-start | bytes 3686400 | tf_op jit(solution)/shard_map/reduce_scatter | solution.py:121
  1042.6 93.4 %copy-start = (f32[2048,400]{0,1:T(8,128)S(1)}, f32[2048,400]{0,1:T(8,128)}, u32[]{:S(2)}) copy-start(f32[2048,400]{0,1:T(8,128)} %all-reduce.3.cloned.1.call-done) | copy-start | bytes 9830404
  1129.4 6.5 copy-start.1
  1129.4 6.5 copy-start.2
  1129.4 6.5 copy-start.3
Sparse Core Ops, SparseCore 0:
  10.2 52.8 all-gather.1
  951.2 91.3 all-reduce.2
  1045.5 37.0 reduce-scatter.1
where the time goes:
time: 1160 us; the launch traced here: 1150 us
  other arithmetic  342 us (29%)
  local copies, waits for them, and re-layouts  295 us (25%)
  blocking collectives  240 us (21%)
  matrix products  130 us (11%)
  waiting for transfers between devices  87.4 us (8%)
  starting transfers between devices  22.7 us (2%)
  between operations  18 us (2%)
  loops' own time  13.4 us (1%)
    psum x1, blocking collectives, body(): total = lax.psum(jnp.sum(counts).astype(jnp.float32), ('rel', 'ent'))  197 us
    gather x2, local copies, waits for them, and re-layouts, body(): hidden = ent_low[sources].astype(jnp.float32) + rel_sum[relation]  87.1 us
    dot_general x2, matrix products, block(): lax.dot_general(hid, rows, (((1,), (1,)), ((), ())), preferred_element_ty...  72.1 us
    scatter-add x1, other arithmetic, body(): ent_grad = ent_grad.at[sources.reshape(-1)].add(returned)  65.2 us
    scatter-add x1, other arithmetic, body(): ent_grad = ent_grad.at[dst_in.reshape(-1)].add(g_target.reshape(-1, width))  63.3 us
    scatter-add x1, other arithmetic, body(): jnp.zeros(rel_sum.shape, jnp.float32).at[relation.reshape(-1)].add(returned)  63.1 us
    scatter-add x1, other arithmetic, body(): ent_grad.at[negatives.reshape(-1)].add(g_negative.reshape(-1, width))  53.3 us
    gather x4, local copies, waits for them, and re-layouts, block(): rows = ent_low[neg]  46.5 us
  transfers between devices with their start and end apart: 7, of which 3 were waited for; matrix products, arithmetic and copies ran while one was open for 30% of the time, Pallas kernels for 0%

commit v1 on v0

--- a/solution.py
+++ b/solution.py
@@ -1,11 +1,18 @@
+import functools
 import math
 
 import jax
 import jax.numpy as jnp
 from jax import lax
+from jax.experimental import pallas as pl
+from jax.experimental.pallas import tpu as pltpu
 from jax.sharding import PartitionSpec as P
 
 STEP = 10
+f32 = jnp.float32
+bf16 = jnp.bfloat16
+i32 = jnp.int32
+MESH = pl.DeviceIdType.MESH
 
 
 margin = 2.5
@@ -29,7 +36,7 @@
     return (weight, moment, second)
 
 
-def body(
+def general_body(
     ent_table,
     entity_first_moment,
     ent_v,
@@ -144,7 +151,609 @@
     )
 
 
+KT1=256
+RP=256
+
+def split3(x):
+    hi=x.astype(bf16).astype(f32); r=x-hi
+    mid=r.astype(bf16).astype(f32); lo=r-mid
+    return hi,mid,lo
+
+def place():
+    r=lax.axis_index("rel"); e=lax.axis_index("ent")
+    z=lax.div(e,2); k=lax.rem(e,2)
+    xn=r+1-2*lax.rem(r,2)
+    yn=lax.rem(r+2,4)
+    return r,z,k,xn,yn
+
+def gather_kernel(et_ref, rt_ref, src_ref, rid_ref, neg_ref,
+                  tab_ref, h_ref, negout_ref,
+                  tb, rall, eh, hb, lsem, hsem, zs, zr, xs, xr, ys, yr, dxs, dxr, dys, dyr, cs, cr, rs, rr, rcs, rcr, ns, nr):
+    width,ents=et_ref.shape
+    nz=4; parts=8
+    CK=ents//4
+    cap=src_ref.shape[1]
+    c,z,k,xn,yn=place()
+    e=2*z+k
+    half=208
+    sib=2*z+1-k
+    def dev(rel,ent): return (rel,ent)
+    bar=pltpu.get_barrier_semaphore()
+    for d in range(1,parts):
+        pl.semaphore_signal(bar,inc=1,device_id=dev(c,lax.rem(e+d,parts)),device_id_type=MESH)
+    pl.semaphore_signal(bar,inc=1,device_id=dev(xn,e),device_id_type=MESH)
+    pl.semaphore_signal(bar,inc=1,device_id=dev(yn,e),device_id_type=MESH)
+    tb[...]=et_ref[...].astype(bf16)
+    rsum=(rt_ref[0]+rt_ref[1])+rt_ref[2] if False else (rt_ref[0].astype(bf16).astype(f32)+rt_ref[1].astype(bf16).astype(f32)+rt_ref[2].astype(bf16).astype(f32))
+    rsum=jnp.concatenate([rsum,jnp.zeros((RP-rsum.shape[0],width),f32)],0)
+    rall[e]=rsum.T.astype(bf16)
+    pl.semaphore_wait(bar,parts+1)
+    def rc(src,dst,s,r,to):
+        return pltpu.make_async_remote_copy(src_ref=src,dst_ref=dst,send_sem=s,recv_sem=r,device_id=to,device_id_type=MESH)
+    lanes=pl.ds(pl.multiple_of(c*CK,CK),CK)
+    lanes_x=pl.ds(pl.multiple_of(xn*CK,CK),CK)
+    lanes_y=pl.ds(pl.multiple_of(yn*CK,CK),CK)
+    def rel_copy(zz,o):
+        return rc(rall.at[2*o+k],rall.at[2*o+k],rs.at[zz],rr.at[o],dev(c,2*zz+k))
+    def rel_sib(o,kk):
+        return rc(rall.at[2*o+kk],rall.at[2*o+kk],rcs.at[o],rcr.at[o],dev(c,sib))
+    for dz in range(1,nz):
+        rel_copy(lax.rem(z+dz,nz),z).start()
+    rel_sib(z,k).start()
+    def neg_copy(to,own):
+        return rc(neg_ref.at[to],negout_ref.at[own],ns.at[to],nr.at[own],dev(c,to))
+    for d in range(1,parts):
+        neg_copy(lax.rem(e+d,parts),e).start()
+    own_neg=pltpu.make_async_copy(neg_ref.at[e],negout_ref.at[e],lsem.at[1])
+    own_neg.start()
+    def up(o,own):
+        src=tb.at[:,lanes] if own else tab_ref.at[2*o+k,:,lanes]
+        return rc(src,tab_ref.at[2*o+k,:,lanes],zs.at[0,o],zr.at[o],dev(c,2*(z+1)+k))
+    def down(o,own):
+        src=tb.at[:,lanes] if own else tab_ref.at[2*o+k,:,lanes]
+        return rc(src,tab_ref.at[2*o+k,:,lanes],zs.at[1,o],zr.at[o],dev(c,2*(z-1)+k))
+    @pl.when(z<nz-1)
+    def _(): up(z,True).start()
+    @pl.when(z>0)
+    def _(): down(z,True).start()
+    own_tab=pltpu.make_async_copy(tb,tab_ref.at[e],lsem.at[0])
+    own_tab.start()
+    def core_copy(o,kk,own):
+        src=tb if own else tab_ref.at[2*o+kk]
+        return rc(src,tab_ref.at[2*o+kk],cs.at[o],cr.at[o],dev(c,sib))
+    core_copy(z,k,True).start()
+    def xcopy(o,l): return rc(tab_ref.at[2*o+k,:,l],tab_ref.at[2*o+k,:,l],xs.at[o],xr.at[o],dev(xn,e))
+    def ycopy(o,l): return rc(tab_ref.at[2*o+k,:,l],tab_ref.at[2*o+k,:,l],ys.at[o],yr.at[o],dev(yn,e))
+    def dycopy(o,l):
+        v=tab_ref.at[2*o+k,0:half,l]
+        return rc(v,v,dys.at[o],dyr.at[o],dev(yn,e))
+    def dxcopy(o,l):
+        v=tab_ref.at[2*o+k,half:width,l]
+        return rc(v,v,dxs.at[o],dxr.at[o],dev(xn,e))
+    def sides(dist,fn):
+        @pl.when(z>=dist)
+        def _(): fn(z-dist,True)
+        @pl.when(z+dist<nz)
+        def _(): fn(z+dist,False)
+    def arrive(dist):
+        def fn(o,below):
+            rc(tb.at[:,lanes],tab_ref.at[2*o+k,:,lanes],zs.at[0,o],zr.at[o],dev(c,e)).wait_recv()
+            if below:
+                @pl.when(z<nz-1)
+                def _(): up(o,False).start()
+            else:
+                @pl.when(z>0)
+                def _(): down(o,False).start()
+            xcopy(o,lanes).start()
+            ycopy(o,lanes).start()
+        sides(dist,fn)
+    def cross(dist):
+        def fn(o,below):
+            xcopy(o,lanes_x).wait_recv()
+            dycopy(o,lanes_x).start()
+            ycopy(o,lanes_y).wait_recv()
+            dxcopy(o,lanes_y).start()
+        sides(dist,fn)
+    def whole(dist):
+        def fn(o,below):
+            l_d=pl.ds(pl.multiple_of((3-c)*CK,CK),CK)
+            dycopy(o,l_d).wait_recv()
+            dxcopy(o,l_d).wait_recv()
+            core_copy(o,k,False).start()
+        sides(dist,fn)
+    def onehot(ids):
+        return jnp.where(lax.broadcasted_iota(i32,(ents,KT1),0)==ids,1.0,0.0).astype(bf16)
+    nt=cap//KT1
+    def src_slot(b):
+        def tile(t,_):
+            l=pl.ds(pl.multiple_of(t*KT1,KT1),KT1)
+            eh[b,:,l]=jnp.dot(tb[...],onehot(src_ref[b:b+1,l]),preferred_element_type=f32).astype(bf16)
+            return 0
+        lax.fori_loop(0,nt,tile,0)
+    def out_copy(b):
+        return pltpu.make_async_copy(hb.at[b%2],h_ref.at[pl.ds(b*cap,cap),:],hsem.at[b%2])
+    nrel=rt_ref.shape[1]
+    def rel_slot(b):
+        if b>=2: out_copy(b-2).wait()
+        def tile(t,_):
+            l=pl.ds(pl.multiple_of(t*KT1,KT1),KT1)
+            q=rid_ref[b:b+1,l]
+            g=jnp.floor((q.astype(f32)+0.5)*(1.0/nrel)).astype(i32)
+            q=q+(RP-nrel)*g
+            acc=eh[b,:,l].astype(f32)
+            for g0 in range(0,parts):
+                oh=jnp.where(lax.broadcasted_iota(i32,(RP,KT1),0)+RP*g0==q,1.0,0.0).astype(bf16)
+                acc=acc+jnp.dot(rall[g0],oh,preferred_element_type=f32)
+            hid=acc.astype(bf16)
+            hf=hid.astype(f32)
+            hi,mid,lo=split3(jnp.sum(hf*hf,0,keepdims=True))
+            row=lax.broadcasted_iota(i32,(hb.shape[2]-width,KT1),0)
+            ex=jnp.where(row==0,hi,jnp.where(row==1,mid,jnp.where(row==2,lo,jnp.where(row<6,1.0,0.0))))
+            hb[b%2,pl.ds(pl.multiple_of(t*KT1,KT1),KT1),:]=jnp.concatenate([hf,ex],0).T.astype(bf16)
+            return 0
+        lax.fori_loop(0,nt,tile,0)
+        out_copy(b).start()
+    for b in range(4): src_slot(b)
+    arrive(1)
+    for b in range(4,6): src_slot(b)
+    for dz in range(1,nz):
+        o=lax.rem(z+dz,nz)
+        rel_copy(z,o).wait_recv()
+        rel_sib(o,k).start()
+    arrive(2)
+    cross(1)
+    for b in range(6,8): src_slot(b)
+    whole(1)
+    for o in range(nz): rel_sib(o,1-k).wait_recv()
+    arrive(3)
+    rel_slot(0); rel_slot(1)
+    cross(2)
+    rel_slot(2); rel_slot(3)
+    whole(2); cross(3)
+    for b in range(4,8): rel_slot(b)
+    whole(3)
+    for o in range(nz): core_copy(o,1-k,False).wait_recv()
+    core_copy(z,k,True).wait_send()
+    for dist in range(1,nz):
+        def fn(o,below):
+            core_copy(o,k,False).wait_send()
+            xcopy(o,lanes).wait_send(); ycopy(o,lanes).wait_send()
+            dycopy(o,lanes_x).wait_send(); dxcopy(o,lanes_y).wait_send()
+            if below:
+                @pl.when(z<nz-1)
+                def _(): up(o,False).wait_send()
+            else:
+                @pl.when(z>0)
+                def _(): down(o,False).wait_send()
+        sides(dist,fn)
+    @pl.when(z<nz-1)
+    def _(): up(z,True).wait_send()
+    @pl.when(z>0)
+    def _(): down(z,True).wait_send()
+    for dz in range(1,nz):
+        o=lax.rem(z+dz,nz)
+        rel_copy(o,z).wait_send()
+    for o in range(nz): rel_sib(o,k).wait_send()
+    for d in range(1,parts):
+        o=lax.rem(e+d,parts)
+        neg_copy(o,e).wait_send()
+        neg_copy(e,o).wait_recv()
+    own_tab.wait(); own_neg.wait()
+    out_copy(6).wait(); out_copy(7).wait()
+
+def gather_call(et,rt,src,rid,negs):
+    width,ents=et.shape
+    parts,cap=src.shape
+    D=pltpu.SemaphoreType.DMA
+    V=pl.BlockSpec(memory_space=pltpu.VMEM); A=pl.BlockSpec(memory_space=pl.ANY)
+    return pl.pallas_call(gather_kernel,name="k1_gather",
+        in_specs=[V]*5,out_specs=[A,A,V],
+        out_shape=[jax.ShapeDtypeStruct((parts,width,ents),bf16),jax.ShapeDtypeStruct((parts*cap,512),bf16),jax.ShapeDtypeStruct(negs.shape,i32)],
+        scratch_shapes=[pltpu.VMEM((width,ents),bf16),pltpu.VMEM((parts,width,RP),bf16),pltpu.VMEM((parts,width,cap),bf16),pltpu.VMEM((2,cap,512),bf16),
+            D((2,)),D((2,)),D((2,4)),D((4,)),D((4,)),D((4,)),D((4,)),D((4,)),D((4,)),D((4,)),D((4,)),D((4,)),D((4,)),D((4,)),D((4,)),D((4,)),D((4,)),D((4,)),D((8,)),D((8,))],
+        compiler_params=pltpu.CompilerParams(collective_id=1,has_side_effects=True,vmem_limit_bytes=60<<20))(et,rt,src,rid,negs)
+
+
+KT = 256
+WA=416
+def block_kernel(width, ents, negcount, CH,
+                 counts_ref, h_ref, t_ref, dst_ref, neg_ref, gh_ref, g_ref, loss_ref,
+                 ta_ref, tr_ref, acc_ref, crow_ref, s_ref):
+    j=pl.program_id(0)
+    wa=ta_ref.shape[0]
+    count=counts_ref[j]
+    tiles=lax.div(count+(KT-1),KT)
+    t=t_ref[0]
+    tf=t.astype(f32)
+    norm=(jnp.sum(tf*tf,0,keepdims=True)+1.0)*0.25
+    hi,mid,lo=split3(norm)
+    ta_ref[0:width,:]=t*bf16(-0.5)
+    sub=lax.broadcasted_iota(jnp.int32,(wa-width,ents),0)
+    pad=jnp.where(sub<3,0.25,0.0)
+    pad=jnp.where(sub==3,hi,pad)
+    pad=jnp.where(sub==4,mid,pad)
+    pad=jnp.where(sub==5,lo,pad)
+    ta_ref[width:,:]=pad.astype(bf16)
+    tcat=jnp.concatenate([t, jnp.where(sub==0,1.0,0.0).astype(bf16)],0)
+    tr_ref[...]=tcat.T
+    ids=neg_ref[0]
+    nn=ids.shape[1]
+    ohi=jnp.where(lax.broadcasted_iota(jnp.int32,(ents//128,nn),0)==lax.shift_right_arithmetic(ids,7),1.0,0.0).astype(bf16)
+    olo=jnp.where(lax.broadcasted_iota(jnp.int32,(128,nn),0)==(ids&127),1.0,0.0).astype(bf16)
+    c=lax.dot_general(ohi,olo,(((1,),(1,)),((),())),preferred_element_type=f32)*(1.0/negcount)
+    for i in range(ents//128):
+        crow_ref[0:1,128*i:128*(i+1)]=c[i:i+1,:]
+    acc_ref[...]=jnp.zeros_like(acc_ref)
+    gh_ref[...]=jnp.zeros_like(gh_ref)
+    @pl.when(j==0)
+    def _(): loss_ref[...]=jnp.zeros_like(loss_ref)
+    first=jnp.logical_and(lax.broadcasted_iota(jnp.int32,(8,128),0)==0,lax.broadcasted_iota(jnp.int32,(8,128),1)==0)
+    loss_ref[8:16,:]+=jnp.where(first,count.astype(f32),0.0)
+    eye=lax.broadcasted_iota(jnp.int32,(KT,KT),0)==lax.broadcasted_iota(jnp.int32,(KT,KT),1)
+    lanes=lax.broadcasted_iota(jnp.int32,(1,CH),1)
+    nch=ents//CH
+    def rows_of(kt): return pl.ds(pl.multiple_of(kt*KT,KT),KT)
+    def live_of(kt): return (lax.broadcasted_iota(jnp.int32,(KT,1),0)+kt*KT)<count
+    def idcol(kt):
+        idr=dst_ref[0,pl.ds(kt,1),:].astype(f32)
+        return jnp.sum(jnp.where(eye,idr,0.0),1,keepdims=True).astype(jnp.int32)
+    def aug(kt):
+        hb=h_ref[rows_of(kt),:]
+        last=hb[:,width//128*128:wa].astype(f32)
+        lane=lax.broadcasted_iota(jnp.int32,last.shape,1)+width//128*128
+        last=jnp.where(jnp.logical_and(lane==width,jnp.logical_not(live_of(kt))),4e6,last)
+        return jnp.concatenate([hb[:,:width//128*128],last.astype(bf16)],1)
+    def sdot(ha,ci): return jnp.dot(ha,ta_ref[:,ci*CH:(ci+1)*CH],preferred_element_type=f32)
+    def post(s,idc,ci,sp):
+        es=jnp.where((idc-ci*CH)==lanes,s,0.0)
+        for a in range(CH//128): sp=sp+es[:,128*a:128*(a+1)]
+        s_ref[:,ci*CH:(ci+1)*CH]=s
+        return sp
+    def column(sp,kt):
+        live=live_of(kt)
+        sq=jnp.sum(sp,1,keepdims=True)*4.0
+        rr=lax.rsqrt(sq)
+        x=sq*rr-margin
+        a=jnp.where(live,jax.nn.sigmoid(x)*rr,0.0)
+        inva=jnp.where(live,1.0/a,0.0)
+        pos=jnp.where(live,jnp.maximum(x,0.0)+jnp.log(1.0+jnp.exp(-jnp.abs(x))),0.0)
+        p8=pos[0:8]
+        for b in range(1,KT//8): p8+=pos[8*b:8*b+8]
+        loss_ref[0:8,:]+=jnp.where(lax.broadcasted_iota(jnp.int32,(8,128),1)==0,p8,0.0)
+        return a,inva
+    ha=aug(0); idc=idcol(0); sp=jnp.zeros((KT,128),f32)
+    for ci in range(nch): sp=post(sdot(ha,ci),idc,ci,sp)
+    a0,i0=column(sp,0)
+    def tile(kt,carry):
+        rho,inva,idc=carry
+        nk=jnp.minimum(kt+1,tiles-1)
+        hb=h_ref[rows_of(kt),:]
+        hf=hb[:,:width].astype(f32)
+        hi,mid,lo=split3(rho)
+        ex=lax.broadcasted_iota(jnp.int32,(KT,wa-width),1)
+        pad=jnp.where(ex==0,hi,jnp.where(ex==1,mid,jnp.where(ex==2,lo,0.0)))
+        hat=jnp.concatenate([(hf*rho),pad],1).astype(bf16).T
+        ha=aug(nk); nidc=idcol(nk)
+        gh=jnp.zeros((KT,wa),f32)
+        sp=jnp.zeros((KT,128),f32)
+        lsum=jnp.zeros((8,CH),f32)
+        ss=[None]*nch; ms=[None]*nch
+        ss[0]=sdot(ha,0)
+        for ci in range(nch+1):
+            if ci+1<nch: ss[ci+1]=sdot(ha,ci+1)
+            if ci>=1:
+                pc=slice((ci-1)*CH,ci*CH)
+                gh+=jnp.dot(ms[ci-1],tr_ref[pc,:],preferred_element_type=f32)
+                acc_ref[:,pc]+=jnp.dot(hat,ms[ci-1],preferred_element_type=f32)
+            if ci<nch:
+                cols=slice(ci*CH,(ci+1)*CH)
+                s=s_ref[:,cols]
+                r=lax.rsqrt(s)
+                th=jnp.tanh(margin*0.5-s*r)
+                mask=(idc-ci*CH)==lanes
+                cr=crow_ref[0:1,cols]
+                x=(cr*0.25*(1.0+th))*(r*inva)
+                ms[ci]=(jnp.where(mask,1.0,0.0)-x).astype(bf16)
+                o=1.0-th
+                p=o[0:8]
+                for b in range(1,KT//8): p=p*o[8*b:8*b+8]
+                lsum+=(math.log(2.0)*(KT//8)-jnp.log(p))*cr
+                sp=post(ss[ci],nidc,ci,sp)
+        l8=lsum[:,0:128]
+        for b in range(1,CH//128): l8+=lsum[:,128*b:128*(b+1)]
+        loss_ref[0:8,:]+=l8
+        out=(hf*gh[:,width:width+1]-gh[:,:width])*rho
+        gh_ref[rows_of(kt),:width]=out.astype(bf16)
+        live=kt+1<tiles
+        na,ni=column(jnp.where(live,sp,1.0),jnp.where(live,nk,tiles))
+        return na,ni,nidc
+    lax.fori_loop(0,tiles,tile,(a0,i0,idc))
+    g_ref[0]=tf*acc_ref[width:width+1,:]+tf*acc_ref[width+1:width+2,:]+tf*acc_ref[width+2:width+3,:]-acc_ref[0:width,:]
+
+def run_blocks(h,tables,dst,neg,counts,negcount,CH=512,approx=True):
+    parts,width,ents=tables.shape
+    cap=h.shape[0]//parts
+    wa=WA
+    nn=neg.shape[-1]
+    gs=pltpu.PrefetchScalarGridSpec(num_scalar_prefetch=1,grid=(parts,),
+      in_specs=[pl.BlockSpec((cap,h.shape[1]),lambda j,c:(j,0)),
+                pl.BlockSpec((1,width,ents),lambda j,c:(j,0,0)),
+                pl.BlockSpec((1,cap//KT,KT),lambda j,c:(j,0,0)),
+                pl.BlockSpec((1,1,nn),lambda j,c:(j,0,0))],
+      out_specs=[pl.BlockSpec((cap,width),lambda j,c:(j,0)),
+                 pl.BlockSpec((1,width,ents),lambda j,c:(j,0,0)),
+                 pl.BlockSpec((16,128),lambda j,c:(0,0))],
+      scratch_shapes=[pltpu.VMEM((wa,ents),bf16),pltpu.VMEM((ents,wa),bf16),
+                      pltpu.VMEM((wa,ents),f32),pltpu.VMEM((8,ents),f32),pltpu.VMEM((KT,ents),f32)])
+    return pl.pallas_call(functools.partial(block_kernel,width,ents,negcount,CH),grid_spec=gs,name="k2_blocks",
+      out_shape=[jax.ShapeDtypeStruct((h.shape[0],width),bf16),jax.ShapeDtypeStruct(tables.shape,f32),jax.ShapeDtypeStruct((16,128),f32)],
+      compiler_params=pltpu.CompilerParams(vmem_limit_bytes=60<<20,dimension_semantics=("arbitrary",)))(counts,h,tables,dst,neg)
+
+
+HALF=208
+BT=bf16
+ZT=bf16
+RT=f32
+
+def reduce_kernel(g_ref, gh_ref, src_ref, rid_ref, sc_ref,
+                  ge_ref, gr_ref, sco_ref,
+                  pr, own, sacc, racc, sax, say, rax, ray, sbx, sby, rbx, rby, sz, rz, ghb, ght, rp, rsz, rzr, scb,
+                  ps, prr, osem, gsem, axs, axr, ays, ayr, bxs, bxr, bys, byr, zs, zr, rps, rpr, rzs, rzrr, gxs, gxr, gys, gyr, gdxs, gdxr, gdys, gdyr, css, csr, czs, czr):
+    parts,width,ents=g_ref.shape
+    nz=4; CK=ents//4
+    cap=src_ref.shape[1]
+    nrel=gr_ref.shape[0]
+    c,z,k,xn,yn=place()
+    e=2*z+k; sib=2*z+1-k
+    x=lax.rem(c,2); y=lax.div(c,2)
+    bar=pltpu.get_barrier_semaphore()
+    for to in ((c,sib),(xn,e),(yn,e))+tuple((c,lax.rem(e+2*d,parts)) for d in range(1,nz)):
+        pl.semaphore_signal(bar,inc=1,device_id=to,device_id_type=MESH)
+    pl.semaphore_wait(bar,nz+2)
+    def rc(src,dst,s,r,to):
+        return pltpu.make_async_remote_copy(src_ref=src,dst_ref=dst,send_sem=s,recv_sem=r,device_id=to,device_id_type=MESH)
+    order=[lax.rem(z+1+i,nz) for i in range(nz)]
+    def pair(i): return rc(g_ref.at[2*order[i]+1-k],pr.at[i],ps.at[i],prr.at[i],(c,sib))
+    def load(i): return pltpu.make_async_copy(g_ref.at[2*order[i]+k],own.at[i%2],osem.at[i%2])
+    for i in range(nz): pair(i).start()
+    load(0).start(); load(1).start()
+    def gload(b): return pltpu.make_async_copy(gh_ref.at[pl.ds(b*cap,cap),:],ghb.at[b%2],gsem.at[b%2])
+    gload(0).start()
+    def lane(ck,n=1): return pl.ds(pl.multiple_of(ck*CK,CK),n*CK)
+    def ax(i): return rc(sax.at[i],rax.at[i],axs.at[i],axr.at[i],(xn,e))
+    def ay(i): return rc(say.at[i],ray.at[i],ays.at[i],ayr.at[i],(yn,e))
+    def bx(i): return rc(sbx.at[i],rbx.at[i],bxs.at[i],bxr.at[i],(xn,e))
+    def by(i): return rc(sby.at[i],rby.at[i],bys.at[i],byr.at[i],(yn,e))
+    def zc(i): return rc(sz.at[i],rz.at[i],zs.at[i],zr.at[i],(c,2*order[i]+k))
+    RB=16
+    def strips(lo,hi,fn):
+        def it(t,_):
+            fn(pl.ds(pl.multiple_of(lo+t*RB,RB),RB),pl.ds(pl.multiple_of(t*RB,RB),RB)); return 0
+        lax.fori_loop(0,(hi-lo)//RB,it,0)
+    xo=1-x; yo=1-y
+    def stage0(i):
+        pair(i).wait_recv()
+        load(i).wait()
+        def one(rows,rel,xfirst):
+            v=pr[i,rows,:]+own[i%2,rows,:]
+            if i==nz-1: v=v+sacc[rows,:]
+            pr[i,rows,:]=v
+        strips(0,HALF,lambda rows,rel: one(rows,rel,True))
+        strips(HALF,width,lambda rows,rel: one(rows,rel,False))
+        def sx(rows,rel):
+            sax[i,rel,0:CK]=pr[i,rows,lane(xo)].astype(bf16)
+            sax[i,rel,CK:]=pr[i,rows,lane(xo+2)].astype(bf16)
+        strips(0,HALF,sx)
+        ax(i).start()
+        def sy(rows,rel):
+            say[i,rel,:]=pr[i,rows,lane(2*yo,2)].astype(bf16)
+        strips(HALF,width,sy)
+        ay(i).start()
+        if i+2<nz: load(i+2).start()
+    def stageB(i):
+        ax(i).wait_recv()
+        def px(rows,rel):
+            sby[i,rel,:]=(pr[i,rows,lane(x+2*yo)]+rax[i,rel,lane(yo)].astype(f32)).astype(BT)
+            pr[i,rows,lane(c)]=pr[i,rows,lane(c)]+rax[i,rel,lane(y)].astype(f32)
+        strips(0,HALF,px)
+        by(i).start()
+        ay(i).wait_recv()
+        def py(rows,rel):
+            sbx[i,rel,:]=(pr[i,rows,lane(2*y+xo)]+ray[i,rel,lane(xo)].astype(f32)).astype(BT)
+            pr[i,rows,lane(c)]=pr[i,rows,lane(c)]+ray[i,rel,lane(x)].astype(f32)
+        strips(HALF,width,py)
+        bx(i).start()
+    def stageZ(i):
+        by(i).wait_recv(); bx(i).wait_recv()
+        last=i==nz-1
+        def one(buf):
+            def f(rows,rel):
+                v=pr[i,rows,lane(c)]+buf[i,rel,:].astype(f32)
+                if last: ge_ref[rows,lane(c)]=v
+                else: sz[i,rows,:]=v.astype(ZT)
+            return f
+        strips(0,HALF,one(rby)); strips(HALF,width,one(rbx))
+        if not last: zc(i).start()
+    def getblock(b):
+        gload(b).wait()
+        if b+1<parts: gload(b+1).start()
+    EC=512
+    def src_slot(b):
+        ght[...]=ghb[b%2].T
+        KT=256
+        eye=lax.broadcasted_iota(i32,(KT,KT),0)==lax.broadcasted_iota(i32,(KT,KT),1)
+        cols=[]
+        for t in range(cap//KT):
+            idr=src_ref[b:b+1,t*KT:(t+1)*KT].astype(f32)
+            cols.append(jnp.sum(jnp.where(eye,idr,0.0),1,keepdims=True).astype(i32))
+        idc=jnp.concatenate(cols,0)
+        def chunk(t,_):
+            l=pl.ds(pl.multiple_of(t*EC,EC),EC)
+            oh=jnp.where(idc==lax.broadcasted_iota(i32,(1,EC),1)+t*EC,1.0,0.0).astype(bf16)
+            d=jnp.dot(ght[...],oh,preferred_element_type=f32)
+            if b==0: sacc[:,l]=d
+            else: sacc[:,l]=sacc[:,l]+d
+            return 0
+        lax.fori_loop(0,ents//EC,chunk,0)
+    QC=nrel*2
+    def rel_slot(b):
+        ids=rid_ref[b:b+1,:]
+        def chunk(t,_):
+            rows=pl.ds(pl.multiple_of(t*QC,8),QC)
+            oh=jnp.where(lax.broadcasted_iota(i32,(QC,cap),0)+t*QC==ids,1.0,0.0).astype(bf16)
+            d=jnp.dot(oh,ghb[b%2],preferred_element_type=f32)
+            if b==0: racc[rows,:]=d
+            else: racc[rows,:]=racc[rows,:]+d
+            return 0
+        lax.fori_loop(0,parts*nrel//QC,chunk,0)
+    def grp(g): return pl.ds(pl.multiple_of(g*nrel,8),nrel)
+    def relpair(i): return rc(racc.at[grp(2*order[i]+1-k),:],rp.at[i],rps.at[i],rpr.at[i],(c,sib))
+    def relz(i): return rc(rsz.at[i],rzr.at[i],rzs.at[i],rzrr.at[i],(c,2*order[i]+k))
+    def slot(b):
+        getblock(b); src_slot(b); rel_slot(b)
+    slot(0)
+    stage0(0)
+    slot(1)
+    stage0(1)
+    stageB(0)
+    slot(2)
+    stage0(2)
+    stageB(1)
+    stageZ(0)
+    slot(3)
+    stageB(2)
+    stageZ(1)
+    slot(4)
+    stageZ(2)
+    for b in range(5,parts): slot(b)
+    stage0(3)
+    for i in range(nz): relpair(i).start()
+    for i in range(nz-1):
+        relpair(i).wait_recv()
+        rsz[i]=(racc[grp(2*order[i]+k),:]+rp[i]).astype(RT)
+        relz(i).start()
+    stageB(3)
+    stageZ(3)
+    for i in range(nz-1):
+        zc(i).wait_recv()
+    def fin(rows,rel):
+        v=ge_ref[rows,lane(c)]
+        for i in range(nz-1): v=v+rz[i,rows,:].astype(f32)
+        ge_ref[rows,lane(c)]=v
+        return v
+    def fit(t,acc):
+        v=fin(pl.ds(pl.multiple_of(t*RB,RB),RB),None)
+        return acc+v*v
+    sq=lax.fori_loop(0,width//RB,fit,jnp.zeros((RB,CK),f32))
+    def gx(l): return rc(ge_ref.at[:,l],ge_ref.at[:,l],gxs,gxr,(xn,e))
+    def gy(l): return rc(ge_ref.at[:,l],ge_ref.at[:,l],gys,gyr,(yn,e))
+    def gdy(l): return rc(ge_ref.at[0:HALF,l],ge_ref.at[0:HALF,l],gdys,gdyr,(yn,e))
+    def gdx(l): return rc(ge_ref.at[HALF:width,l],ge_ref.at[HALF:width,l],gdxs,gdxr,(xn,e))
+    gx(lane(c)).start(); gy(lane(c)).start()
+    relpair(nz-1).wait_recv()
+    rv=racc[grp(e),:]+rp[nz-1]
+    for i in range(nz-1):
+        relz(i).wait_recv()
+        rv=rv+rzr[i].astype(f32)
+    gr_ref[...]=rv
+    one=jnp.sum(sq)+3.0*jnp.sum(rv*rv)
+    row=lax.broadcasted_iota(i32,(8,128),0)
+    v=jnp.where(row==0,one,jnp.where(row==1,jnp.sum(sc_ref[0:8,:]),jnp.where(row==2,jnp.sum(sc_ref[8:16,:]),0.0)))
+    for s,to in enumerate(((c,sib),(xn,e),(yn,e))):
+        scb[s]=v
+        cp=rc(scb.at[s],scb.at[3+s],css.at[s],csr.at[s],to)
+        cp.start(); cp.wait()
+        v=v+scb[3+s]
+        if s==1:
+            gx(lane(xn)).wait_recv(); gdy(lane(xn)).start()
+            gy(lane(yn)).wait_recv(); gdx(lane(yn)).start()
+    scb[6+z]=v
+    def cz(d): return rc(scb.at[6+z],scb.at[6+z],czs.at[d],czr.at[d],(c,lax.rem(e+2*d,parts)))
+    for d in range(1,nz): cz(d).start()
+    for d in range(1,nz): cz(d).wait()
+    sco_ref[...]=(scb[6]+scb[7])+(scb[8]+scb[9])
+    gdy(lane(3-c)).wait_recv(); gdx(lane(3-c)).wait_recv()
+    gx(lane(c)).wait_send(); gy(lane(c)).wait_send(); gdy(lane(xn)).wait_send(); gdx(lane(yn)).wait_send()
+    for i in range(nz):
+        pair(i).wait_send(); ax(i).wait_send(); ay(i).wait_send(); bx(i).wait_send(); by(i).wait_send(); relpair(i).wait_send()
+        if i<nz-1: zc(i).wait_send(); relz(i).wait_send()
+
+def reduce_call(g,gh,src,rid,sc,nrel):
+    parts,width,ents=g.shape
+    cap=src.shape[1]; nz=4; CK=ents//4
+    D=pltpu.SemaphoreType.DMA
+    V=pl.BlockSpec(memory_space=pltpu.VMEM); A=pl.BlockSpec(memory_space=pl.ANY)
+    VM=pltpu.VMEM
+    return pl.pallas_call(reduce_kernel,name="k3_reduce",
+        in_specs=[A,A,V,V,V],out_specs=[V,V,V],
+        out_shape=[jax.ShapeDtypeStruct((width,ents),f32),jax.ShapeDtypeStruct((nrel,width),f32),jax.ShapeDtypeStruct((8,128),f32)],
+        scratch_shapes=[VM((nz,width,ents),f32),VM((2,width,ents),f32),VM((width,ents),f32),VM((parts*nrel,width),f32),
+            VM((nz,HALF,2*CK),bf16),VM((nz,width-HALF,2*CK),bf16),VM((nz,HALF,2*CK),bf16),VM((nz,width-HALF,2*CK),bf16),
+            VM((nz,width-HALF,CK),BT),VM((nz,HALF,CK),BT),VM((nz,width-HALF,CK),BT),VM((nz,HALF,CK),BT),
+            VM((nz-1,width,CK),ZT),VM((nz-1,width,CK),ZT),
+            VM((2,cap,width),bf16),VM((width,cap),bf16),VM((nz,nrel,width),f32),VM((nz-1,nrel,width),RT),VM((nz-1,nrel,width),RT),VM((10,8,128),f32),
+            D((4,)),D((4,)),D((2,)),D((2,)),D((4,)),D((4,)),D((4,)),D((4,)),D((4,)),D((4,)),D((4,)),D((4,)),D((3,)),D((3,)),D((4,)),D((4,)),D((3,)),D((3,)),
+            D,D,D,D,D,D,D,D,D((3,)),D((3,)),D((4,)),D((4,))],
+        compiler_params=pltpu.CompilerParams(collective_id=2,has_side_effects=True,vmem_limit_bytes=62<<20))(g,gh,src,rid,sc)
+
+
+def cube_body(
+    ent_table,
+    entity_first_moment,
+    ent_v,
+    rel_table,
+    relation_first_moment,
+    rel_v,
+    src_ids,
+    rel_ids,
+    dst_ids,
+    neg_ids,
+    bucket_counts,
+):
+    parts, slots = src_ids.shape[2:]
+    negcount = neg_ids.shape[3]
+    nrel = rel_table.shape[1]
+    clip_level = 0.01 / math.sqrt(lax.axis_size("rel") * lax.axis_size("ent") * parts * slots)
+    padded = -(-negcount // 1024) * 1024
+    negs = jnp.pad(neg_ids[0, 0], ((0, 0), (0, padded - negcount)), constant_values=-1)
+    tables, hidden, arrived = gather_call(
+        ent_table.T, rel_table, src_ids[0, 0], rel_ids[0, 0], negs.reshape(parts, -1, 128)
+    )
+    back, partial, sums = run_blocks(
+        hidden,
+        tables,
+        dst_ids[0, 0].reshape(parts, -1, KT),
+        arrived.reshape(parts, 1, padded),
+        bucket_counts[0, 0],
+        negcount,
+    )
+    ent_grad, rel_grad, totals = reduce_call(
+        partial, back, src_ids[0, 0], rel_ids[0, 0], sums, nrel
+    )
+    squares, loss_sum, total = totals[0, 0], totals[1, 0], totals[2, 0]
+    grad_norm = jnp.sqrt(squares) / total
+    scale = jnp.minimum(1.0, clip_level / grad_norm) / total
+    new_ent, new_ent_m, new_ent_v = adamw(ent_table, entity_first_moment, ent_v, scale * ent_grad.T)
+    new_rel, new_rel_m, new_rel_v = adamw(
+        rel_table, relation_first_moment, rel_v, scale * rel_grad[None]
+    )
+    return (
+        loss_sum,
+        total,
+        grad_norm,
+        new_ent,
+        new_ent_m,
+        new_ent_v,
+        new_ent.astype(jnp.bfloat16),
+        new_rel,
+        new_rel_m,
+        new_rel_v,
+        new_rel.astype(jnp.bfloat16),
+    )
+
+
 def solution(mesh):
+    body = cube_body if mesh.shape["rel"] == 4 and mesh.shape["ent"] == 8 else general_body
     return jax.shard_map(
         body,
         mesh=mesh,

time: 1160 us -> 371 us (0.32)
  Pallas kernels: 0 us -> 343 us
  other arithmetic: 342 us -> 12.3 us
  local copies, waits for them, and re-layouts: 295 us -> 4.47 us
  blocking collectives: 240 us -> 0 us
  matrix products: 130 us -> 0 us
  waiting for transfers between devices: 87.4 us -> 0 us
  starting transfers between devices: 22.7 us -> 0 us
  between operations: 18 us -> 4.59 us
  loops' own time: 13.4 us -> 0 us
    pallas_call x0 -> x3, Pallas kernels: none -> 343 us  [the longest x1 143 us: reduce_call(): pl.pallas_call(reduce_kernel, name='k3_reduce', in_specs=[A, A, V, V, V],...]
    scatter-add x4 -> x0, other arithmetic: 245 us -> none  [the longest x1 65.2 us: body(): ent_grad = ent_grad.at[sources.reshape(-1)].add(returned)]
    psum x2 -> x0, blocking collectives: 240 us -> none  [the longest x1 197 us: body(): total = lax.psum(jnp.sum(counts).astype(jnp.float32), ('rel', 'ent'))]
    gather x8 -> x0, local copies, waits for them, and re-layouts: 176 us -> none  [the longest x2 87.1 us: body(): hidden = ent_low[sources].astype(jnp.float32) + rel_sum[relation]]
    dot_general x6 -> x0, matrix products: 130 us -> none  [the longest x2 72.1 us: block(): lax.dot_general(hid, rows, (((1,), (1,)), ((), ())), preferred_element_ty...]
    convert_element_type x6 -> x0, local copies, waits for them, and re-layouts: 70.8 us -> none  [the longest x4 42 us: block(): diff = hid_f - ent_low[dst].astype(jnp.float32)]
    reduce_scatter x1 -> x0, waiting for transfers between devices: 35.8 us -> none  [body(): lax.psum_scatter(rel_local, 'ent', scatter_dimension=0, tiled=True)]
    another operation x4 -> x1, local copies, waits for them, and re-layouts: 35.4 us -> 1.43 us  [cube_body(): dst_ids[0, 0].reshape(parts, -1, KT)]
  transfers between devices with their start and end apart: 7 -> 0, of which waited for: 3 -> 0; matrix products, arithmetic and copies ran while one was open for 30% -> 0% of each run, Pallas kernels for 0% -> 0%
where the time goes in v1:
time: 371 us; the launch traced here: 365 us
  Pallas kernels  343 us (92%)
  other arithmetic  12.3 us (3%)
  between operations  4.59 us (1%)
  local copies, waits for them, and re-layouts  4.47 us (1%)
    pallas_call x1, Pallas kernels, reduce_call(): pl.pallas_call(reduce_kernel, name='k3_reduce', in_specs=[A, A, V, V, V],...  143 us
    pallas_call x1, Pallas kernels, run_blocks(): pl.pallas_call(functools.partial(block_kernel, width, ents, negcount, CH)...  101 us
    pallas_call x1, Pallas kernels, gather_call(): pl.pallas_call(gather_kernel, name='k1_gather', in_specs=[V] * 5, out_spe...  99.4 us

profile of v1, /device:TPU:8, one launch (start us, length us, event | category | flops | bytes accessed | tf_op | source)
XLA Modules:
  0.0 364.8 jit_solution(9899038671741632894)
XLA Ops:
  0.6 0.8 pad_bitcast_fusion
  1.4 0.6 copy.25
  2.0 1.4 copy.22.dst_ref
  3.5 99.4 %k1_gather.1 = (bf16[8,400,2048]{2,1,0:T(8,128)(2,1)}, bf16[10240,512]{1,0:T(8,128)(2,1)}, s32[8,8,128]{2,1,0:T(8,128)}) custom-call(f32[400,2048]{1,0:T(8,128)} %bitcast.22, f32[3,200,400]{2,1,0:T(8,128)} %rt_ref.1, s32[8,1280]{1,0:T(8,128)} %bitcast.23, s32[8,1280]{1,0:T(8,128)} %bitcast.25, s32[8,8,128]{2,1,0:T(8,128)} %bitcast.27), custom_call_target="tpu_custom_call" | custom-call | tf_op jit(solution)/shard_map/k1_gather/pallas_call | solution.py:349
  102.8 101.1 %k2_blocks.1 = (bf16[10240,400]{1,0:T(8,128)(2,1)}, f32[8,400,2048]{2,1,0:T(8,128)}, f32[16,128]{1,0:T(8,128)}) custom-call(s32[8]{0:T(128)} %bitcast.31, bf16[10240,512]{1,0:T(8,128)(2,1)} %get-tuple-element.20.h_ref, bf16[8,400,2048]{2,1,0:T(8,128)(2,1)} %get-tuple-element.21.t_ref, s32[8,5,256]{2,1,0:T(8,128)} %copy.22.dst_ref, s32[8,1,1024]{2,1,0:T(1,128)} %bitcast.29), custom_call_target="tpu_custom_call" | custom-call | tf_op jit(solution)/shard_map/k2_blocks/pallas_call | solution.py:488
  203.9 0.0 copy-start.1
  203.9 143.0 %k3_reduce.1 = (f32[400,2048]{1,0:T(8,128)}, f32[200,400]{1,0:T(8,128)}, f32[8,128]{1,0:T(8,128)}) custom-call(f32[8,400,2048]{2,1,0:T(8,128)} %get-tuple-element.23.g_ref, bf16[10240,400]{1,0:T(8,128)(2,1)} %get-tuple-element.24.gh_ref, s32[8,1280]{1,0:T(8,128)} %bitcast.24, s32[8,1280]{1,0:T(8,128)} %bitcast.26, f32[16,128]{1,0:T(8,128)} %get-tuple-element.25.sc_ref), custom_call_target="tpu_custom_call" | custom-call | tf_op jit(solution)/shard_map/k3_reduce/pallas_call | solution.py:687
  346.9 1.3 fusion.6
  350.9 0.0 copy-start.3
  351.0 1.3 multiply_multiply_fusion.1
  352.2 0.0 copy-done.1
  352.2 0.0 copy-start
  352.2 0.0 copy-start.2
  352.3 4.4 %fusion.2 = (bf16[3,200,400]{2,1,0:T(8,128)(2,1)}, f32[3,200,400]{2,1,0:T(8,128)}, f32[3,200,400]{2,1,0:T(8,128)}, f32[3,200,400]{2,1,0:T(8,128)}) fusion(f32[3,200,400]{2,1,0:T(8,128)S(1)} %copy-done.1, f32[200,400]{1,0:T(8,128)S(1)} %get-tuple-element.38, f32[3,200,400]{2,1,0:T(8,128)} %param.15, f32[200,400]{1,0:T(8,128)S(1)} %get-tuple-element.37, ...), kind=kLoop, calls=%fused_computation.12 | loop fusion | flops 3120000 | bytes 6880000 | tf_op jit(solution)/shard_map/convert_element_type | solution.py:751
  356.7 0.0 copy-done.3
  356.7 0.0 copy-done
  356.7 0.3 copy-done.2
  357.0 6.6 %fusion.3 = (bf16[2048,400]{0,1:T(8,128)(2,1)}, f32[2048,400]{0,1:T(8,128)}, f32[2048,400]{0,1:T(8,128)}, f32[2048,400]{0,1:T(8,128)}) fusion(f32[2048,400]{0,1:T(8,128)S(1)} %copy-done, f32[400,2048]{1,0:T(8,128)} %get-tuple-element.27, f32[]{:T(128)S(6)} %div.41, f32[2048,400]{0,1:T(8,128)S(1)} %copy-done.2, f32[2048,400]{0,1:T(8,128)S(1)} %copy-done.3), kind=kLoop, calls=%fused_computation.13 | loop fusion | flops 13926400 | bytes 24576004 | tf_op jit(solution)/shard_map/convert_element_type | solution.py:747
Async XLA Ops:
  203.9 148.3 %copy-start.1 = (f32[3,200,400]{2,1,0:T(8,128)S(1)}, f32[3,200,400]{2,1,0:T(8,128)}, u32[]{:S(2)}) copy-start(f32[3,200,400]{2,1,0:T(8,128)} %rt_ref.1) | copy-start | bytes 2880004
  350.9 5.7 %copy-start.3 = (f32[2048,400]{0,1:T(8,128)S(1)}, f32[2048,400]{0,1:T(8,128)}, u32[]{:S(2)}) copy-start(f32[2048,400]{0,1:T(8,128)} %param.13) | copy-start | bytes 9830404
  352.2 4.5 %copy-start = (f32[2048,400]{0,1:T(8,128)S(1)}, f32[2048,400]{0,1:T(8,128)}, u32[]{:S(2)}) copy-start(f32[2048,400]{0,1:T(8,128)} %param.11) | copy-start | bytes 9830404
  352.2 4.8 %copy-start.2 = (f32[2048,400]{0,1:T(8,128)S(1)}, f32[2048,400]{0,1:T(8,128)}, u32[]{:S(2)}) copy-start(f32[2048,400]{0,1:T(8,128)} %param.12) | copy-start | bytes 9830404

commit v2 on v1

--- a/solution.py
+++ b/solution.py
@@ -168,7 +168,7 @@
 
 def gather_kernel(et_ref, rt_ref, src_ref, rid_ref, neg_ref,
                   tab_ref, h_ref, negout_ref,
-                  tb, rall, eh, hb, lsem, hsem, zs, zr, xs, xr, ys, yr, dxs, dxr, dys, dyr, cs, cr, rs, rr, rcs, rcr, ns, nr):
+                  tb, rall, eh, hb, lsem, hsem, us, ds, zr, xs, xr, ys, yr, fs, fr, cs, cr, rcs, rcr, ns, nr):
     width,ents=et_ref.shape
     nz=4; parts=8
     CK=ents//4
@@ -177,89 +177,80 @@
     e=2*z+k
     half=208
     sib=2*z+1-k
-    def dev(rel,ent): return (rel,ent)
     bar=pltpu.get_barrier_semaphore()
     for d in range(1,parts):
-        pl.semaphore_signal(bar,inc=1,device_id=dev(c,lax.rem(e+d,parts)),device_id_type=MESH)
-    pl.semaphore_signal(bar,inc=1,device_id=dev(xn,e),device_id_type=MESH)
-    pl.semaphore_signal(bar,inc=1,device_id=dev(yn,e),device_id_type=MESH)
+        pl.semaphore_signal(bar,inc=1,device_id=(c,lax.rem(e+d,parts)),device_id_type=MESH)
+    pl.semaphore_signal(bar,inc=1,device_id=(xn,e),device_id_type=MESH)
+    pl.semaphore_signal(bar,inc=1,device_id=(yn,e),device_id_type=MESH)
     tb[...]=et_ref[...].astype(bf16)
-    rsum=(rt_ref[0]+rt_ref[1])+rt_ref[2] if False else (rt_ref[0].astype(bf16).astype(f32)+rt_ref[1].astype(bf16).astype(f32)+rt_ref[2].astype(bf16).astype(f32))
-    rsum=jnp.concatenate([rsum,jnp.zeros((RP-rsum.shape[0],width),f32)],0)
+    low=[rt_ref[l].astype(bf16).astype(f32) for l in range(3)]
+    rsum=jnp.concatenate([low[0]+low[1]+low[2],jnp.zeros((RP-rt_ref.shape[1],width),f32)],0)
     rall[e]=rsum.T.astype(bf16)
     pl.semaphore_wait(bar,parts+1)
     def rc(src,dst,s,r,to):
         return pltpu.make_async_remote_copy(src_ref=src,dst_ref=dst,send_sem=s,recv_sem=r,device_id=to,device_id_type=MESH)
-    lanes=pl.ds(pl.multiple_of(c*CK,CK),CK)
-    lanes_x=pl.ds(pl.multiple_of(xn*CK,CK),CK)
-    lanes_y=pl.ds(pl.multiple_of(yn*CK,CK),CK)
-    def rel_copy(zz,o):
-        return rc(rall.at[2*o+k],rall.at[2*o+k],rs.at[zz],rr.at[o],dev(c,2*zz+k))
+    rows_of=(pl.ds(0,half),pl.ds(half,width-half))
+    def lane(ck): return pl.ds(pl.multiple_of(ck*CK,CK),CK)
+    SEQ=((2,1),(0,1),(2,2),(1,1),(2,3),(0,2),(1,2),(0,3),(1,3))
+    def part(o,u,own=False):
+        if u==2: return rall.at[2*o+k]
+        return tb.at[rows_of[u],lane(c)] if own else tab_ref.at[2*o+k,rows_of[u],lane(c)]
+    def up(o,u,own): return rc(part(o,u,own),part(o,u),us.at[u,o],zr.at[u,o],(c,2*(z+1)+k))
+    def down(o,u,own): return rc(part(o,u,own),part(o,u),ds.at[u,o],zr.at[u,o],(c,2*(z-1)+k))
+    def sides(dist,fn):
+        @pl.when(z>=dist)
+        def _(): fn(z-dist)
+        @pl.when(z+dist<nz)
+        def _(): fn(z+dist)
+    def along(n,act):
+        u,dist=SEQ[n]
+        f=dist-1
+        @pl.when(jnp.logical_and(z<nz-1,z>=f))
+        def _(): act(up(z-f,u,f==0))
+        @pl.when(jnp.logical_and(z>0,z+f<nz))
+        def _(): act(down(z+f,u,f==0))
+    def xc(o,h,l): return rc(tab_ref.at[2*o+k,rows_of[h],l],tab_ref.at[2*o+k,rows_of[h],l],xs.at[o,h],xr.at[o,h],(xn,e))
+    def yc(o,h,l): return rc(tab_ref.at[2*o+k,rows_of[h],l],tab_ref.at[2*o+k,rows_of[h],l],ys.at[o,h],yr.at[o,h],(yn,e))
+    def fc(o,h,l):
+        v=tab_ref.at[2*o+k,rows_of[h],l]
+        return rc(v,v,fs.at[o,h],fr.at[o,h],((yn,e),(xn,e))[h])
+    def cc(o,h,kk,own=False):
+        v=tab_ref.at[2*o+kk,rows_of[h],:]
+        return rc(tb.at[rows_of[h],:] if own else v,v,cs.at[o,h],cr.at[o,h],(c,sib))
     def rel_sib(o,kk):
-        return rc(rall.at[2*o+kk],rall.at[2*o+kk],rcs.at[o],rcr.at[o],dev(c,sib))
-    for dz in range(1,nz):
-        rel_copy(lax.rem(z+dz,nz),z).start()
+        return rc(rall.at[2*o+kk],rall.at[2*o+kk],rcs.at[o],rcr.at[o],(c,sib))
+    along(0,lambda cp: cp.start())
+    along(1,lambda cp: cp.start())
     rel_sib(z,k).start()
     def neg_copy(to,own):
-        return rc(neg_ref.at[to],negout_ref.at[own],ns.at[to],nr.at[own],dev(c,to))
+        return rc(neg_ref.at[to],negout_ref.at[own],ns.at[to],nr.at[own],(c,to))
     for d in range(1,parts):
         neg_copy(lax.rem(e+d,parts),e).start()
     own_neg=pltpu.make_async_copy(neg_ref.at[e],negout_ref.at[e],lsem.at[1])
     own_neg.start()
-    def up(o,own):
-        src=tb.at[:,lanes] if own else tab_ref.at[2*o+k,:,lanes]
-        return rc(src,tab_ref.at[2*o+k,:,lanes],zs.at[0,o],zr.at[o],dev(c,2*(z+1)+k))
-    def down(o,own):
-        src=tb.at[:,lanes] if own else tab_ref.at[2*o+k,:,lanes]
-        return rc(src,tab_ref.at[2*o+k,:,lanes],zs.at[1,o],zr.at[o],dev(c,2*(z-1)+k))
-    @pl.when(z<nz-1)
-    def _(): up(z,True).start()
-    @pl.when(z>0)
-    def _(): down(z,True).start()
     own_tab=pltpu.make_async_copy(tb,tab_ref.at[e],lsem.at[0])
     own_tab.start()
-    def core_copy(o,kk,own):
-        src=tb if own else tab_ref.at[2*o+kk]
-        return rc(src,tab_ref.at[2*o+kk],cs.at[o],cr.at[o],dev(c,sib))
-    core_copy(z,k,True).start()
-    def xcopy(o,l): return rc(tab_ref.at[2*o+k,:,l],tab_ref.at[2*o+k,:,l],xs.at[o],xr.at[o],dev(xn,e))
-    def ycopy(o,l): return rc(tab_ref.at[2*o+k,:,l],tab_ref.at[2*o+k,:,l],ys.at[o],yr.at[o],dev(yn,e))
-    def dycopy(o,l):
-        v=tab_ref.at[2*o+k,0:half,l]
-        return rc(v,v,dys.at[o],dyr.at[o],dev(yn,e))
-    def dxcopy(o,l):
-        v=tab_ref.at[2*o+k,half:width,l]
-        return rc(v,v,dxs.at[o],dxr.at[o],dev(xn,e))
-    def sides(dist,fn):
-        @pl.when(z>=dist)
-        def _(): fn(z-dist,True)
-        @pl.when(z+dist<nz)
-        def _(): fn(z+dist,False)
-    def arrive(dist):
-        def fn(o,below):
-            rc(tb.at[:,lanes],tab_ref.at[2*o+k,:,lanes],zs.at[0,o],zr.at[o],dev(c,e)).wait_recv()
-            if below:
-                @pl.when(z<nz-1)
-                def _(): up(o,False).start()
+    for h in range(2): cc(z,h,k,True).start()
+    def Z(n):
+        u,dist=SEQ[n]
+        def fn(o):
+            up(o,u,False).wait_recv()
+            if u==2: rel_sib(o,k).start()
             else:
-                @pl.when(z>0)
-                def _(): down(o,False).start()
-            xcopy(o,lanes).start()
-            ycopy(o,lanes).start()
+                xc(o,u,lane(c)).start(); yc(o,u,lane(c)).start()
         sides(dist,fn)
-    def cross(dist):
-        def fn(o,below):
-            xcopy(o,lanes_x).wait_recv()
-            dycopy(o,lanes_x).start()
-            ycopy(o,lanes_y).wait_recv()
-            dxcopy(o,lanes_y).start()
+        if n+2<len(SEQ): along(n+2,lambda cp: cp.start())
+    def C(dist,h):
+        def fn(o):
+            if h==0: xc(o,0,lane(xn)).wait_recv(); fc(o,0,lane(xn)).start()
+            else: yc(o,1,lane(yn)).wait_recv(); fc(o,1,lane(yn)).start()
         sides(dist,fn)
-    def whole(dist):
-        def fn(o,below):
-            l_d=pl.ds(pl.multiple_of((3-c)*CK,CK),CK)
-            dycopy(o,l_d).wait_recv()
-            dxcopy(o,l_d).wait_recv()
-            core_copy(o,k,False).start()
+    def W(dist,h):
+        def fn(o):
+            if h==0: yc(o,0,lane(yn)).wait_recv()
+            else: xc(o,1,lane(xn)).wait_recv()
+            fc(o,h,lane(3-c)).wait_recv()
+            cc(o,h,k).start()
         sides(dist,fn)
     def onehot(ids):
         return jnp.where(lax.broadcasted_iota(i32,(ents,KT1),0)==ids,1.0,0.0).astype(bf16)
@@ -293,46 +284,56 @@
             return 0
         lax.fori_loop(0,nt,tile,0)
         out_copy(b).start()
-    for b in range(4): src_slot(b)
-    arrive(1)
-    for b in range(4,6): src_slot(b)
-    for dz in range(1,nz):
-        o=lax.rem(z+dz,nz)
-        rel_copy(z,o).wait_recv()
-        rel_sib(o,k).start()
-    arrive(2)
-    cross(1)
-    for b in range(6,8): src_slot(b)
-    whole(1)
-    for o in range(nz): rel_sib(o,1-k).wait_recv()
-    arrive(3)
-    rel_slot(0); rel_slot(1)
-    cross(2)
-    rel_slot(2); rel_slot(3)
-    whole(2); cross(3)
-    for b in range(4,8): rel_slot(b)
-    whole(3)
-    for o in range(nz): core_copy(o,1-k,False).wait_recv()
-    core_copy(z,k,True).wait_send()
-    for dist in range(1,nz):
-        def fn(o,below):
-            core_copy(o,k,False).wait_send()
-            xcopy(o,lanes).wait_send(); ycopy(o,lanes).wait_send()
-            dycopy(o,lanes_x).wait_send(); dxcopy(o,lanes_y).wait_send()
-            if below:
-                @pl.when(z<nz-1)
-                def _(): up(o,False).wait_send()
-            else:
-                @pl.when(z>0)
-                def _(): down(o,False).wait_send()
-        sides(dist,fn)
-    @pl.when(z<nz-1)
-    def _(): up(z,True).wait_send()
-    @pl.when(z>0)
-    def _(): down(z,True).wait_send()
-    for dz in range(1,nz):
-        o=lax.rem(z+dz,nz)
-        rel_copy(o,z).wait_send()
+    def allrel():
+        for o in range(nz): rel_sib(o,1-k).wait_recv()
+    src_slot(0)
+    src_slot(1)
+    Z(0)
+    src_slot(2)
+    Z(1)
+    src_slot(3)
+    Z(2)
+    src_slot(4)
+    C(1,0)
+    src_slot(5)
+    Z(3)
+    src_slot(6)
+    Z(4)
+    W(1,0)
+    src_slot(7)
+    C(1,1)
+    Z(5)
+    allrel()
+    rel_slot(0)
+    W(1,1)
+    Z(6)
+    rel_slot(1)
+    C(2,0)
+    Z(7)
+    rel_slot(2)
+    W(2,0)
+    C(2,1)
+    Z(8)
+    rel_slot(3)
+    W(2,1)
+    C(3,0)
+    rel_slot(4)
+    C(3,1)
+    W(3,0)
+    rel_slot(5)
+    W(3,1)
+    rel_slot(6)
+    rel_slot(7)
+    for n in range(len(SEQ)): along(n,lambda cp: cp.wait_send())
+    for h in range(2):
+        for o in range(nz): cc(o,h,1-k).wait_recv()
+        cc(z,h,k,True).wait_send()
+        for dist in range(1,nz):
+            def fn(o):
+                cc(o,h,k).wait_send()
+                xc(o,h,lane(c)).wait_send(); yc(o,h,lane(c)).wait_send()
+                fc(o,h,(lane(xn),lane(yn))[h]).wait_send()
+            sides(dist,fn)
     for o in range(nz): rel_sib(o,k).wait_send()
     for d in range(1,parts):
         o=lax.rem(e+d,parts)
@@ -350,7 +351,7 @@
         in_specs=[V]*5,out_specs=[A,A,V],
         out_shape=[jax.ShapeDtypeStruct((parts,width,ents),bf16),jax.ShapeDtypeStruct((parts*cap,512),bf16),jax.ShapeDtypeStruct(negs.shape,i32)],
         scratch_shapes=[pltpu.VMEM((width,ents),bf16),pltpu.VMEM((parts,width,RP),bf16),pltpu.VMEM((parts,width,cap),bf16),pltpu.VMEM((2,cap,512),bf16),
-            D((2,)),D((2,)),D((2,4)),D((4,)),D((4,)),D((4,)),D((4,)),D((4,)),D((4,)),D((4,)),D((4,)),D((4,)),D((4,)),D((4,)),D((4,)),D((4,)),D((4,)),D((4,)),D((8,)),D((8,))],
+            D((2,)),D((2,)),D((3,4)),D((3,4)),D((3,4)),D((4,2)),D((4,2)),D((4,2)),D((4,2)),D((4,2)),D((4,2)),D((4,2)),D((4,2)),D((4,)),D((4,)),D((8,)),D((8,))],
         compiler_params=pltpu.CompilerParams(collective_id=1,has_side_effects=True,vmem_limit_bytes=60<<20))(et,rt,src,rid,negs)
 
 
@@ -380,7 +381,7 @@
     nn=ids.shape[1]
     ohi=jnp.where(lax.broadcasted_iota(jnp.int32,(ents//128,nn),0)==lax.shift_right_arithmetic(ids,7),1.0,0.0).astype(bf16)
     olo=jnp.where(lax.broadcasted_iota(jnp.int32,(128,nn),0)==(ids&127),1.0,0.0).astype(bf16)
-    c=lax.dot_general(ohi,olo,(((1,),(1,)),((),())),preferred_element_type=f32)*(1.0/negcount)
+    c=lax.dot_general(ohi,olo,(((1,),(1,)),((),())),preferred_element_type=f32)
     for i in range(ents//128):
         crow_ref[0:1,128*i:128*(i+1)]=c[i:i+1,:]
     acc_ref[...]=jnp.zeros_like(acc_ref)
@@ -405,7 +406,7 @@
         return jnp.concatenate([hb[:,:width//128*128],last.astype(bf16)],1)
     def sdot(ha,ci): return jnp.dot(ha,ta_ref[:,ci*CH:(ci+1)*CH],preferred_element_type=f32)
     def post(s,idc,ci,sp):
-        es=jnp.where((idc-ci*CH)==lanes,s,0.0)
+        es=jnp.where(idc==lanes+ci*CH,s,0.0)
         for a in range(CH//128): sp=sp+es[:,128*a:128*(a+1)]
         s_ref[:,ci*CH:(ci+1)*CH]=s
         return sp
@@ -437,31 +438,32 @@
         gh=jnp.zeros((KT,wa),f32)
         sp=jnp.zeros((KT,128),f32)
         lsum=jnp.zeros((8,CH),f32)
-        ss=[None]*nch; ms=[None]*nch
-        ss[0]=sdot(ha,0)
+        ms=[None]*nch
+        invn=inva*(0.25/negcount)
+        pend=None
         for ci in range(nch+1):
-            if ci+1<nch: ss[ci+1]=sdot(ha,ci+1)
-            if ci>=1:
-                pc=slice((ci-1)*CH,ci*CH)
-                gh+=jnp.dot(ms[ci-1],tr_ref[pc,:],preferred_element_type=f32)
-                acc_ref[:,pc]+=jnp.dot(hat,ms[ci-1],preferred_element_type=f32)
             if ci<nch:
                 cols=slice(ci*CH,(ci+1)*CH)
                 s=s_ref[:,cols]
                 r=lax.rsqrt(s)
                 th=jnp.tanh(margin*0.5-s*r)
-                mask=(idc-ci*CH)==lanes
+                sp=post(sdot(ha,ci),nidc,ci,sp)
                 cr=crow_ref[0:1,cols]
-                x=(cr*0.25*(1.0+th))*(r*inva)
-                ms[ci]=(jnp.where(mask,1.0,0.0)-x).astype(bf16)
+                mask=idc==lanes+ci*CH
+                u=(1.0+th).astype(bf16)
+                x=(u*cr.astype(bf16))*(r*invn).astype(bf16)
+                ms[ci]=jnp.where(mask,1.0,0.0).astype(bf16)-x
                 o=1.0-th
                 p=o[0:8]
                 for b in range(1,KT//8): p=p*o[8*b:8*b+8]
                 lsum+=(math.log(2.0)*(KT//8)-jnp.log(p))*cr
-                sp=post(ss[ci],nidc,ci,sp)
+            if ci>=1:
+                pc=slice((ci-1)*CH,ci*CH)
+                gh+=jnp.dot(ms[ci-1],tr_ref[pc,:],preferred_element_type=f32)
+                acc_ref[:,pc]+=jnp.dot(hat,ms[ci-1],preferred_element_type=f32)
         l8=lsum[:,0:128]
         for b in range(1,CH//128): l8+=lsum[:,128*b:128*(b+1)]
-        loss_ref[0:8,:]+=l8
+        loss_ref[0:8,:]+=l8*(1.0/negcount)
         out=(hf*gh[:,width:width+1]-gh[:,:width])*rho
         gh_ref[rows_of(kt),:width]=out.astype(bf16)
         live=kt+1<tiles
@@ -470,7 +472,7 @@
     lax.fori_loop(0,tiles,tile,(a0,i0,idc))
     g_ref[0]=tf*acc_ref[width:width+1,:]+tf*acc_ref[width+1:width+2,:]+tf*acc_ref[width+2:width+3,:]-acc_ref[0:width,:]
 
-def run_blocks(h,tables,dst,neg,counts,negcount,CH=512,approx=True):
+def run_blocks(h,tables,dst,neg,counts,negcount,CH=256):
     parts,width,ents=tables.shape
     cap=h.shape[0]//parts
     wa=WA
@@ -491,168 +493,158 @@
 
 
 HALF=208
-BT=bf16
-ZT=bf16
-RT=f32
 
 def reduce_kernel(g_ref, gh_ref, src_ref, rid_ref, sc_ref,
                   ge_ref, gr_ref, sco_ref,
-                  pr, own, sacc, racc, sax, say, rax, ray, sbx, sby, rbx, rby, sz, rz, ghb, ght, rp, rsz, rzr, scb,
-                  ps, prr, osem, gsem, axs, axr, ays, ayr, bxs, bxr, bys, byr, zs, zr, rps, rpr, rzs, rzrr, gxs, gxr, gys, gyr, gdxs, gdxr, gdys, gdyr, css, csr, czs, czr):
+                  pr, own, sacc, racc, sa0, sa1, ra0, ra1, sb0, sb1, rb0, rb1, sz, rz, ghb, rp, rsz, rzr, scb,
+                  ps, prr, osem, gsem, sas, sar, sbs, sbr, zs, zr, rps, rpr, rzs, rzrr, gxs, gxr, gys, gyr, gds, gdr, css, csr, czs, czr):
     parts,width,ents=g_ref.shape
-    nz=4; CK=ents//4
+    nz=4; CK=ents//4; last=nz-1
     cap=src_ref.shape[1]
     nrel=gr_ref.shape[0]
     c,z,k,xn,yn=place()
     e=2*z+k; sib=2*z+1-k
-    x=lax.rem(c,2); y=lax.div(c,2)
+    x=lax.rem(c,2); y=lax.div(c,2); xo=1-x; yo=1-y
     bar=pltpu.get_barrier_semaphore()
     for to in ((c,sib),(xn,e),(yn,e))+tuple((c,lax.rem(e+2*d,parts)) for d in range(1,nz)):
         pl.semaphore_signal(bar,inc=1,device_id=to,device_id_type=MESH)
+    order=[lax.rem(z+1+i,nz) for i in range(nz)]
+    rows_of=(pl.ds(0,HALF),pl.ds(HALF,width-HALF))
+    lo=(0,HALF); num=(HALF,width-HALF)
+    def load(i): return pltpu.make_async_copy(g_ref.at[2*order[i]+k],own.at[i%2],osem.at[i%2])
+    def gload(b): return pltpu.make_async_copy(gh_ref.at[pl.ds(b*cap,cap),:],ghb.at[b%2],gsem.at[b%2])
+    gload(0).start(); load(0).start(); load(1).start()
     pl.semaphore_wait(bar,nz+2)
     def rc(src,dst,s,r,to):
         return pltpu.make_async_remote_copy(src_ref=src,dst_ref=dst,send_sem=s,recv_sem=r,device_id=to,device_id_type=MESH)
-    order=[lax.rem(z+1+i,nz) for i in range(nz)]
-    def pair(i): return rc(g_ref.at[2*order[i]+1-k],pr.at[i],ps.at[i],prr.at[i],(c,sib))
-    def load(i): return pltpu.make_async_copy(g_ref.at[2*order[i]+k],own.at[i%2],osem.at[i%2])
-    for i in range(nz): pair(i).start()
-    load(0).start(); load(1).start()
-    def gload(b): return pltpu.make_async_copy(gh_ref.at[pl.ds(b*cap,cap),:],ghb.at[b%2],gsem.at[b%2])
-    gload(0).start()
+    def pair(i,h): return rc(g_ref.at[2*order[i]+1-k,rows_of[h],:],pr.at[i,rows_of[h],:],ps.at[i,h],prr.at[i,h],(c,sib))
+    for i in range(2):
+        for h in range(2): pair(i,h).start()
     def lane(ck,n=1): return pl.ds(pl.multiple_of(ck*CK,CK),n*CK)
-    def ax(i): return rc(sax.at[i],rax.at[i],axs.at[i],axr.at[i],(xn,e))
-    def ay(i): return rc(say.at[i],ray.at[i],ays.at[i],ayr.at[i],(yn,e))
-    def bx(i): return rc(sbx.at[i],rbx.at[i],bxs.at[i],bxr.at[i],(xn,e))
-    def by(i): return rc(sby.at[i],rby.at[i],bys.at[i],byr.at[i],(yn,e))
-    def zc(i): return rc(sz.at[i],rz.at[i],zs.at[i],zr.at[i],(c,2*order[i]+k))
+    near=((xn,e),(yn,e)); sa=(sa0,sa1); ra=(ra0,ra1); sb=(sb0,sb1); rb=(rb0,rb1)
+    def ac(i,h): return rc(sa[h].at[i],ra[h].at[i],sas.at[i,h],sar.at[i,h],near[h])
+    def bc(i,h): return rc(sb[h].at[i],rb[h].at[i],sbs.at[i,h],sbr.at[i,h],near[1-h])
+    def zc(i,h): return rc(sz.at[i,rows_of[h],:],rz.at[i,rows_of[h],:],zs.at[i,h],zr.at[i,h],(c,2*order[i]+k))
+    gone=((xo,xo+2),(2*yo,2*yo+1))
+    kept=((x,x+2),(2*y,2*y+1))
+    passed=(x+2*yo,2*y+xo)
+    mine=(y,x)
     RB=16
-    def strips(lo,hi,fn):
-        def it(t,_):
-            fn(pl.ds(pl.multiple_of(lo+t*RB,RB),RB),pl.ds(pl.multiple_of(t*RB,RB),RB)); return 0
-        lax.fori_loop(0,(hi-lo)//RB,it,0)
-    xo=1-x; yo=1-y
-    def stage0(i):
-        pair(i).wait_recv()
-        load(i).wait()
-        def one(rows,rel,xfirst):
-            v=pr[i,rows,:]+own[i%2,rows,:]
-            if i==nz-1: v=v+sacc[rows,:]
-            pr[i,rows,:]=v
-        strips(0,HALF,lambda rows,rel: one(rows,rel,True))
-        strips(HALF,width,lambda rows,rel: one(rows,rel,False))
-        def sx(rows,rel):
-            sax[i,rel,0:CK]=pr[i,rows,lane(xo)].astype(bf16)
-            sax[i,rel,CK:]=pr[i,rows,lane(xo+2)].astype(bf16)
-        strips(0,HALF,sx)
-        ax(i).start()
-        def sy(rows,rel):
-            say[i,rel,:]=pr[i,rows,lane(2*yo,2)].astype(bf16)
-        strips(HALF,width,sy)
-        ay(i).start()
-        if i+2<nz: load(i+2).start()
-    def stageB(i):
-        ax(i).wait_recv()
-        def px(rows,rel):
-            sby[i,rel,:]=(pr[i,rows,lane(x+2*yo)]+rax[i,rel,lane(yo)].astype(f32)).astype(BT)
-            pr[i,rows,lane(c)]=pr[i,rows,lane(c)]+rax[i,rel,lane(y)].astype(f32)
-        strips(0,HALF,px)
-        by(i).start()
-        ay(i).wait_recv()
-        def py(rows,rel):
-            sbx[i,rel,:]=(pr[i,rows,lane(2*y+xo)]+ray[i,rel,lane(xo)].astype(f32)).astype(BT)
-            pr[i,rows,lane(c)]=pr[i,rows,lane(c)]+ray[i,rel,lane(x)].astype(f32)
-        strips(HALF,width,py)
-        bx(i).start()
-    def stageZ(i):
-        by(i).wait_recv(); bx(i).wait_recv()
-        last=i==nz-1
-        def one(buf):
-            def f(rows,rel):
-                v=pr[i,rows,lane(c)]+buf[i,rel,:].astype(f32)
-                if last: ge_ref[rows,lane(c)]=v
-                else: sz[i,rows,:]=v.astype(ZT)
-            return f
-        strips(0,HALF,one(rby)); strips(HALF,width,one(rbx))
-        if not last: zc(i).start()
+    def strips(h,fn):
+        fn(rows_of[h],pl.ds(0,num[h]))
+    def st0(i,h):
+        if h==0 and i!=last: load(i).wait()
+        pair(i,h).wait_recv()
+        def one(rows,rel):
+            for s in range(2):
+                l=lane(gone[h][s])
+                sa[h][i,rel,s*CK:(s+1)*CK]=(pr[i,rows,l]+own[i%2,rows,l]).astype(bf16)
+                l=lane(kept[h][s])
+                pr[i,rows,l]=pr[i,rows,l]+own[i%2,rows,l]
+        strips(h,one)
+        ac(i,h).start()
+        if h==1 and i+2<nz:
+            load(i+2).start()
+            for g in range(2): pair(i+2,g).start()
+    def stB(i,h):
+        ac(i,h).wait_recv()
+        def one(rows,rel):
+            sb[h][i,rel,:]=(pr[i,rows,lane(passed[h])]+ra[h][i,rel,lane(1-mine[h])].astype(f32)).astype(sb0.dtype)
+            pr[i,rows,lane(c)]=pr[i,rows,lane(c)]+ra[h][i,rel,lane(mine[h])].astype(f32)
+        strips(h,one)
+        bc(i,h).start()
+    def stZ(i,h):
+        bc(i,h).wait_recv()
+        def one(rows,rel):
+            v=pr[i,rows,lane(c)]+rb[h][i,rel,:].astype(f32)
+            if i==last: ge_ref[rows,lane(c)]=v
+            else: sz[i,rows,:]=v.astype(sz.dtype)
+        strips(h,one)
+        if i!=last: zc(i,h).start()
+    def both(fn,i):
+        fn(i,0); fn(i,1)
     def getblock(b):
         gload(b).wait()
-        if b+1<parts: gload(b+1).start()
-    EC=512
-    def src_slot(b):
-        ght[...]=ghb[b%2].T
-        KT=256
-        eye=lax.broadcasted_iota(i32,(KT,KT),0)==lax.broadcasted_iota(i32,(KT,KT),1)
-        cols=[]
-        for t in range(cap//KT):
-            idr=src_ref[b:b+1,t*KT:(t+1)*KT].astype(f32)
-            cols.append(jnp.sum(jnp.where(eye,idr,0.0),1,keepdims=True).astype(i32))
-        idc=jnp.concatenate(cols,0)
+        gload((b+1)%parts).start()
+    def slot(ids_ref,acc,b,RC):
+        ids=ids_ref[b:b+1,:]
         def chunk(t,_):
-            l=pl.ds(pl.multiple_of(t*EC,EC),EC)
-            oh=jnp.where(idc==lax.broadcasted_iota(i32,(1,EC),1)+t*EC,1.0,0.0).astype(bf16)
-            d=jnp.dot(ght[...],oh,preferred_element_type=f32)
-            if b==0: sacc[:,l]=d
-            else: sacc[:,l]=sacc[:,l]+d
+            rows=pl.ds(pl.multiple_of(t*RC,8),RC)
+            oh=jnp.where(lax.broadcasted_iota(i32,(RC,cap),0)==ids-t*RC,1.0,0.0).astype(bf16)
+            d=jnp.dot(oh,ghb[b%2],preferred_element_type=f32)
+            if b==0: acc[rows,:]=d
+            else: acc[rows,:]=acc[rows,:]+d
             return 0
-        lax.fori_loop(0,ents//EC,chunk,0)
-    QC=nrel*2
-    def rel_slot(b):
-        ids=rid_ref[b:b+1,:]
-        def chunk(t,_):
-            rows=pl.ds(pl.multiple_of(t*QC,8),QC)
-            oh=jnp.where(lax.broadcasted_iota(i32,(QC,cap),0)+t*QC==ids,1.0,0.0).astype(bf16)
-            d=jnp.dot(oh,ghb[b%2],preferred_element_type=f32)
-            if b==0: racc[rows,:]=d
-            else: racc[rows,:]=racc[rows,:]+d
+        lax.fori_loop(0,acc.shape[0]//RC,chunk,0)
+    def src(b):
+        getblock(b); slot(src_ref,sacc,b,CK)
+    def rel(b):
+        getblock(b); slot(rid_ref,racc,b,2*nrel)
+    def addsrc():
+        def it(t,_):
+            l=pl.ds(pl.multiple_of(t*128,128),128)
+            own[last%2,:,l]=own[last%2,:,l]+sacc[l,:].T
             return 0
-        lax.fori_loop(0,parts*nrel//QC,chunk,0)
+        lax.fori_loop(0,ents//128,it,0)
     def grp(g): return pl.ds(pl.multiple_of(g*nrel,8),nrel)
     def relpair(i): return rc(racc.at[grp(2*order[i]+1-k),:],rp.at[i],rps.at[i],rpr.at[i],(c,sib))
     def relz(i): return rc(rsz.at[i],rzr.at[i],rzs.at[i],rzrr.at[i],(c,2*order[i]+k))
-    def slot(b):
-        getblock(b); src_slot(b); rel_slot(b)
-    slot(0)
-    stage0(0)
-    slot(1)
-    stage0(1)
-    stageB(0)
-    slot(2)
-    stage0(2)
-    stageB(1)
-    stageZ(0)
-    slot(3)
-    stageB(2)
-    stageZ(1)
-    slot(4)
-    stageZ(2)
-    for b in range(5,parts): slot(b)
-    stage0(3)
+    src(0)
+    src(1)
+    both(st0,0)
+    src(2)
+    src(3)
+    both(st0,1)
+    src(4)
+    both(stB,0)
+    src(5)
+    src(6)
+    both(st0,2)
+    src(7)
+    load(last).wait()
+    addsrc()
+    both(stB,1)
+    both(stZ,0)
+    rel(0)
+    rel(1)
+    both(st0,3)
+    rel(2)
+    both(stB,2)
+    both(stZ,1)
+    rel(3)
+    rel(4)
+    rel(5)
+    both(stB,3)
+    rel(6)
+    both(stZ,2)
+    rel(7)
+    gload(0).wait()
     for i in range(nz): relpair(i).start()
-    for i in range(nz-1):
+    for i in range(last):
         relpair(i).wait_recv()
-        rsz[i]=(racc[grp(2*order[i]+k),:]+rp[i]).astype(RT)
+        rsz[i]=(racc[grp(2*order[i]+k),:]+rp[i]).astype(rsz.dtype)
         relz(i).start()
-    stageB(3)
-    stageZ(3)
-    for i in range(nz-1):
-        zc(i).wait_recv()
-    def fin(rows,rel):
+    both(stZ,3)
+    sq=jnp.zeros((RB,CK),f32)
+    def gx(h,l): return rc(ge_ref.at[rows_of[h],l],ge_ref.at[rows_of[h],l],gxs.at[h],gxr.at[h],(xn,e))
+    def gy(h,l): return rc(ge_ref.at[rows_of[h],l],ge_ref.at[rows_of[h],l],gys.at[h],gyr.at[h],(yn,e))
+    def gd(h,l): return rc(ge_ref.at[rows_of[h],l],ge_ref.at[rows_of[h],l],gds.at[h],gdr.at[h],near[1-h])
+    for h in range(2):
+        for i in range(last): zc(i,h).wait_recv()
+        rows=rows_of[h]
         v=ge_ref[rows,lane(c)]
-        for i in range(nz-1): v=v+rz[i,rows,:].astype(f32)
+        for i in range(last): v=v+rz[i,rows,:].astype(f32)
         ge_ref[rows,lane(c)]=v
-        return v
-    def fit(t,acc):
-        v=fin(pl.ds(pl.multiple_of(t*RB,RB),RB),None)
-        return acc+v*v
-    sq=lax.fori_loop(0,width//RB,fit,jnp.zeros((RB,CK),f32))
-    def gx(l): return rc(ge_ref.at[:,l],ge_ref.at[:,l],gxs,gxr,(xn,e))
-    def gy(l): return rc(ge_ref.at[:,l],ge_ref.at[:,l],gys,gyr,(yn,e))
-    def gdy(l): return rc(ge_ref.at[0:HALF,l],ge_ref.at[0:HALF,l],gdys,gdyr,(yn,e))
-    def gdx(l): return rc(ge_ref.at[HALF:width,l],ge_ref.at[HALF:width,l],gdxs,gdxr,(xn,e))
-    gx(lane(c)).start(); gy(lane(c)).start()
-    relpair(nz-1).wait_recv()
-    rv=racc[grp(e),:]+rp[nz-1]
-    for i in range(nz-1):
+        v=v*v
+        for b in range(0,num[h],RB): sq=sq+v[b:b+RB]
+        if h==0: gx(0,lane(c)).start()
+        else: gy(1,lane(c)).start()
+    gy(0,lane(c)).start(); gx(1,lane(c)).start()
+    gx(0,lane(xn)).wait_recv(); gd(0,lane(xn)).start()
+    gy(1,lane(yn)).wait_recv(); gd(1,lane(yn)).start()
+    relpair(last).wait_recv()
+    rv=racc[grp(e),:]+rp[last]
+    for i in range(last):
         relz(i).wait_recv()
         rv=rv+rzr[i].astype(f32)
     gr_ref[...]=rv
@@ -664,36 +656,40 @@
         cp=rc(scb.at[s],scb.at[3+s],css.at[s],csr.at[s],to)
         cp.start(); cp.wait()
         v=v+scb[3+s]
-        if s==1:
-            gx(lane(xn)).wait_recv(); gdy(lane(xn)).start()
-            gy(lane(yn)).wait_recv(); gdx(lane(yn)).start()
     scb[6+z]=v
     def cz(d): return rc(scb.at[6+z],scb.at[6+z],czs.at[d],czr.at[d],(c,lax.rem(e+2*d,parts)))
     for d in range(1,nz): cz(d).start()
     for d in range(1,nz): cz(d).wait()
     sco_ref[...]=(scb[6]+scb[7])+(scb[8]+scb[9])
-    gdy(lane(3-c)).wait_recv(); gdx(lane(3-c)).wait_recv()
-    gx(lane(c)).wait_send(); gy(lane(c)).wait_send(); gdy(lane(xn)).wait_send(); gdx(lane(yn)).wait_send()
+    gx(1,lane(xn)).wait_recv(); gy(0,lane(yn)).wait_recv()
+    gd(0,lane(3-c)).wait_recv(); gd(1,lane(3-c)).wait_recv()
+    for h in range(2):
+        gx(h,lane(c)).wait_send(); gy(h,lane(c)).wait_send()
+        for i in range(nz):
+            pair(i,h).wait_send(); ac(i,h).wait_send(); bc(i,h).wait_send()
+            if i<last: zc(i,h).wait_send()
+    gd(0,lane(xn)).wait_send(); gd(1,lane(yn)).wait_send()
     for i in range(nz):
-        pair(i).wait_send(); ax(i).wait_send(); ay(i).wait_send(); bx(i).wait_send(); by(i).wait_send(); relpair(i).wait_send()
-        if i<nz-1: zc(i).wait_send(); relz(i).wait_send()
-
-def reduce_call(g,gh,src,rid,sc,nrel):
+        relpair(i).wait_send()
+        if i<last: relz(i).wait_send()
+
+def reduce_call(g,gh,src,rid,sc,nrel,BT=bf16,ZT=bf16,RT=bf16):
     parts,width,ents=g.shape
     cap=src.shape[1]; nz=4; CK=ents//4
     D=pltpu.SemaphoreType.DMA
     V=pl.BlockSpec(memory_space=pltpu.VMEM); A=pl.BlockSpec(memory_space=pl.ANY)
     VM=pltpu.VMEM
+    rest=width-HALF
     return pl.pallas_call(reduce_kernel,name="k3_reduce",
         in_specs=[A,A,V,V,V],out_specs=[V,V,V],
         out_shape=[jax.ShapeDtypeStruct((width,ents),f32),jax.ShapeDtypeStruct((nrel,width),f32),jax.ShapeDtypeStruct((8,128),f32)],
-        scratch_shapes=[VM((nz,width,ents),f32),VM((2,width,ents),f32),VM((width,ents),f32),VM((parts*nrel,width),f32),
-            VM((nz,HALF,2*CK),bf16),VM((nz,width-HALF,2*CK),bf16),VM((nz,HALF,2*CK),bf16),VM((nz,width-HALF,2*CK),bf16),
-            VM((nz,width-HALF,CK),BT),VM((nz,HALF,CK),BT),VM((nz,width-HALF,CK),BT),VM((nz,HALF,CK),BT),
+        scratch_shapes=[VM((nz,width,ents),f32),VM((2,width,ents),f32),VM((ents,width),f32),VM((parts*nrel,width),f32),
+            VM((nz,HALF,2*CK),bf16),VM((nz,rest,2*CK),bf16),VM((nz,HALF,2*CK),bf16),VM((nz,rest,2*CK),bf16),
+            VM((nz,HALF,CK),BT),VM((nz,rest,CK),BT),VM((nz,HALF,CK),BT),VM((nz,rest,CK),BT),
             VM((nz-1,width,CK),ZT),VM((nz-1,width,CK),ZT),
-            VM((2,cap,width),bf16),VM((width,cap),bf16),VM((nz,nrel,width),f32),VM((nz-1,nrel,width),RT),VM((nz-1,nrel,width),RT),VM((10,8,128),f32),
-            D((4,)),D((4,)),D((2,)),D((2,)),D((4,)),D((4,)),D((4,)),D((4,)),D((4,)),D((4,)),D((4,)),D((4,)),D((3,)),D((3,)),D((4,)),D((4,)),D((3,)),D((3,)),
-            D,D,D,D,D,D,D,D,D((3,)),D((3,)),D((4,)),D((4,))],
+            VM((2,cap,width),bf16),VM((nz,nrel,width),f32),VM((nz-1,nrel,width),RT),VM((nz-1,nrel,width),RT),VM((10,8,128),f32),
+            D((4,2)),D((4,2)),D((2,)),D((2,)),D((4,2)),D((4,2)),D((4,2)),D((4,2)),D((3,2)),D((3,2)),D((4,)),D((4,)),D((3,)),D((3,)),
+            D((2,)),D((2,)),D((2,)),D((2,)),D((2,)),D((2,)),D((3,)),D((3,)),D((4,)),D((4,))],
         compiler_params=pltpu.CompilerParams(collective_id=2,has_side_effects=True,vmem_limit_bytes=62<<20))(g,gh,src,rid,sc)
 
 

time: 371 us -> 319 us (0.86); the launches traced: 365 us -> 317 us
  Pallas kernels: 343 us -> 296 us
    pallas_call x1, Pallas kernels: 143 us -> 123 us  [reduce_call(): pl.pallas_call(reduce_kernel, name='k3_reduce', in_specs=[A, A, V, V, V],...]
    pallas_call x1, Pallas kernels: 99.4 us -> 84.5 us  [gather_call(): pl.pallas_call(gather_kernel, name='k1_gather', in_specs=[V] * 5, out_spe...]
    pallas_call x1, Pallas kernels: 101 us -> 88.7 us  [run_blocks(): pl.pallas_call(functools.partial(block_kernel, width, ents, negcount, CH)...]
where the time goes in v2:
time: 319 us; the launch traced here: 317 us
  Pallas kernels  296 us (93%)
  other arithmetic  12.3 us (4%)
  between operations  4.59 us (1%)
  local copies, waits for them, and re-layouts  4.47 us (1%)
    pallas_call x1, Pallas kernels, reduce_call(): pl.pallas_call(reduce_kernel, name='k3_reduce', in_specs=[A, A, V, V, V],...  123 us
    pallas_call x1, Pallas kernels, run_blocks(): pl.pallas_call(functools.partial(block_kernel, width, ents, negcount, CH)...  88.7 us
    pallas_call x1, Pallas kernels, gather_call(): pl.pallas_call(gather_kernel, name='k1_gather', in_specs=[V] * 5, out_spe...  84.5 us
    convert_element_type x1, other arithmetic, cube_body(): new_ent.astype(jnp.bfloat16)  6.61 us

profile of v2, /device:TPU:8, one launch (start us, length us, event | category | flops | bytes accessed | tf_op | source)
XLA Modules:
  0.0 317.4 jit_solution(5472887475170124155)
XLA Ops:
  0.6 0.8 pad_bitcast_fusion
  1.4 0.6 copy.25
  2.0 1.4 copy.22.dst_ref
  3.5 84.5 %k1_gather.1 = (bf16[8,400,2048]{2,1,0:T(8,128)(2,1)}, bf16[10240,512]{1,0:T(8,128)(2,1)}, s32[8,8,128]{2,1,0:T(8,128)}) custom-call(f32[400,2048]{1,0:T(8,128)} %bitcast.22, f32[3,200,400]{2,1,0:T(8,128)} %rt_ref.1, s32[8,1280]{1,0:T(8,128)} %bitcast.23, s32[8,1280]{1,0:T(8,128)} %bitcast.25, s32[8,8,128]{2,1,0:T(8,128)} %bitcast.27), custom_call_target="tpu_custom_call" | custom-call | tf_op jit(solution)/shard_map/k1_gather/pallas_call | solution.py:350
  87.9 88.7 %k2_blocks.1 = (bf16[10240,400]{1,0:T(8,128)(2,1)}, f32[8,400,2048]{2,1,0:T(8,128)}, f32[16,128]{1,0:T(8,128)}) custom-call(s32[8]{0:T(128)} %bitcast.31, bf16[10240,512]{1,0:T(8,128)(2,1)} %get-tuple-element.20.h_ref, bf16[8,400,2048]{2,1,0:T(8,128)(2,1)} %get-tuple-element.21.t_ref, s32[8,5,256]{2,1,0:T(8,128)} %copy.22.dst_ref, s32[8,1,1024]{2,1,0:T(1,128)} %bitcast.29), custom_call_target="tpu_custom_call" | custom-call | tf_op jit(solution)/shard_map/k2_blocks/pallas_call | solution.py:490
  176.7 0.0 copy-start.1
  176.7 122.8 %k3_reduce.1 = (f32[400,2048]{1,0:T(8,128)}, f32[200,400]{1,0:T(8,128)}, f32[8,128]{1,0:T(8,128)}) custom-call(f32[8,400,2048]{2,1,0:T(8,128)} %get-tuple-element.23.g_ref, bf16[10240,400]{1,0:T(8,128)(2,1)} %get-tuple-element.24.gh_ref, s32[8,1280]{1,0:T(8,128)} %bitcast.24, s32[8,1280]{1,0:T(8,128)} %bitcast.26, f32[16,128]{1,0:T(8,128)} %get-tuple-element.25.sc_ref), custom_call_target="tpu_custom_call" | custom-call | tf_op jit(solution)/shard_map/k3_reduce/pallas_call | solution.py:683
  299.5 1.3 fusion.6
  303.5 0.0 copy-start.3
  303.6 1.3 multiply_multiply_fusion.1
  304.8 0.0 copy-done.1
  304.8 0.0 copy-start
  304.8 0.0 copy-start.2
  304.9 4.4 %fusion.2 = (bf16[3,200,400]{2,1,0:T(8,128)(2,1)}, f32[3,200,400]{2,1,0:T(8,128)}, f32[3,200,400]{2,1,0:T(8,128)}, f32[3,200,400]{2,1,0:T(8,128)}) fusion(f32[3,200,400]{2,1,0:T(8,128)S(1)} %copy-done.1, f32[200,400]{1,0:T(8,128)S(1)} %get-tuple-element.38, f32[3,200,400]{2,1,0:T(8,128)} %param.15, f32[200,400]{1,0:T(8,128)S(1)} %get-tuple-element.37, ...), kind=kLoop, calls=%fused_computation.12 | loop fusion | flops 3120000 | bytes 6880000 | tf_op jit(solution)/shard_map/convert_element_type | solution.py:747
  309.3 0.0 copy-done.3
  309.3 0.0 copy-done
  309.3 0.3 copy-done.2
  309.6 6.6 %fusion.3 = (bf16[2048,400]{0,1:T(8,128)(2,1)}, f32[2048,400]{0,1:T(8,128)}, f32[2048,400]{0,1:T(8,128)}, f32[2048,400]{0,1:T(8,128)}) fusion(f32[2048,400]{0,1:T(8,128)S(1)} %copy-done, f32[400,2048]{1,0:T(8,128)} %get-tuple-element.27, f32[]{:T(128)S(6)} %div.41, f32[2048,400]{0,1:T(8,128)S(1)} %copy-done.2, f32[2048,400]{0,1:T(8,128)S(1)} %copy-done.3), kind=kLoop, calls=%fused_computation.13 | loop fusion | flops 13926400 | bytes 24576004 | tf_op jit(solution)/shard_map/convert_element_type | solution.py:743
Async XLA Ops:
  176.7 128.2 %copy-start.1 = (f32[3,200,400]{2,1,0:T(8,128)S(1)}, f32[3,200,400]{2,1,0:T(8,128)}, u32[]{:S(2)}) copy-start(f32[3,200,400]{2,1,0:T(8,128)} %rt_ref.1) | copy-start | bytes 2880004
  303.5 5.7 %copy-start.3 = (f32[2048,400]{0,1:T(8,128)S(1)}, f32[2048,400]{0,1:T(8,128)}, u32[]{:S(2)}) copy-start(f32[2048,400]{0,1:T(8,128)} %param.13) | copy-start | bytes 9830404
  304.8 4.5 %copy-start = (f32[2048,400]{0,1:T(8,128)S(1)}, f32[2048,400]{0,1:T(8,128)}, u32[]{:S(2)}) copy-start(f32[2048,400]{0,1:T(8,128)} %param.11) | copy-start | bytes 9830404
  304.8 4.8 %copy-start.2 = (f32[2048,400]{0,1:T(8,128)S(1)}, f32[2048,400]{0,1:T(8,128)}, u32[]{:S(2)}) copy-start(f32[2048,400]{0,1:T(8,128)} %param.12) | copy-start | bytes 9830404

commit v3 on v2

--- a/solution.py
+++ b/solution.py
@@ -359,7 +359,7 @@
 WA=416
 def block_kernel(width, ents, negcount, CH,
                  counts_ref, h_ref, t_ref, dst_ref, neg_ref, gh_ref, g_ref, loss_ref,
-                 ta_ref, tr_ref, acc_ref, crow_ref, s_ref):
+                 ta_ref, tr_ref, acc_ref, crow_ref, s_ref, lane_ref):
     j=pl.program_id(0)
     wa=ta_ref.shape[0]
     count=counts_ref[j]
@@ -385,13 +385,16 @@
     for i in range(ents//128):
         crow_ref[0:1,128*i:128*(i+1)]=c[i:i+1,:]
     acc_ref[...]=jnp.zeros_like(acc_ref)
-    gh_ref[...]=jnp.zeros_like(gh_ref)
+    def dead(kt,_):
+        gh_ref[pl.ds(pl.multiple_of(kt*KT,KT),KT),:]=jnp.zeros((KT,gh_ref.shape[1]),bf16)
+        return 0
+    lax.fori_loop(tiles,gh_ref.shape[0]//KT,dead,0)
     @pl.when(j==0)
     def _(): loss_ref[...]=jnp.zeros_like(loss_ref)
     first=jnp.logical_and(lax.broadcasted_iota(jnp.int32,(8,128),0)==0,lax.broadcasted_iota(jnp.int32,(8,128),1)==0)
     loss_ref[8:16,:]+=jnp.where(first,count.astype(f32),0.0)
     eye=lax.broadcasted_iota(jnp.int32,(KT,KT),0)==lax.broadcasted_iota(jnp.int32,(KT,KT),1)
-    lanes=lax.broadcasted_iota(jnp.int32,(1,CH),1)
+    lane_ref[...]=lax.broadcasted_iota(jnp.int32,lane_ref.shape,1)
     nch=ents//CH
     def rows_of(kt): return pl.ds(pl.multiple_of(kt*KT,KT),KT)
     def live_of(kt): return (lax.broadcasted_iota(jnp.int32,(KT,1),0)+kt*KT)<count
@@ -406,7 +409,7 @@
         return jnp.concatenate([hb[:,:width//128*128],last.astype(bf16)],1)
     def sdot(ha,ci): return jnp.dot(ha,ta_ref[:,ci*CH:(ci+1)*CH],preferred_element_type=f32)
     def post(s,idc,ci,sp):
-        es=jnp.where(idc==lanes+ci*CH,s,0.0)
+        es=jnp.where(idc==lane_ref[0:1,ci*CH:(ci+1)*CH],s,0.0)
         for a in range(CH//128): sp=sp+es[:,128*a:128*(a+1)]
         s_ref[:,ci*CH:(ci+1)*CH]=s
         return sp
@@ -438,6 +441,7 @@
         gh=jnp.zeros((KT,wa),f32)
         sp=jnp.zeros((KT,128),f32)
         lsum=jnp.zeros((8,CH),f32)
+        rs=jnp.zeros((KT,128),f32)
         ms=[None]*nch
         invn=inva*(0.25/negcount)
         pend=None
@@ -449,10 +453,10 @@
                 th=jnp.tanh(margin*0.5-s*r)
                 sp=post(sdot(ha,ci),nidc,ci,sp)
                 cr=crow_ref[0:1,cols]
-                mask=idc==lanes+ci*CH
-                u=(1.0+th).astype(bf16)
-                x=(u*cr.astype(bf16))*(r*invn).astype(bf16)
-                ms[ci]=jnp.where(mask,1.0,0.0).astype(bf16)-x
+                mask=idc==lane_ref[0:1,cols]
+                xf=((1.0+th)*cr)*(r*invn)
+                for b in range(CH//128): rs=rs+xf[:,128*b:128*(b+1)]
+                ms[ci]=(jnp.where(mask,1.0,0.0)-xf).astype(bf16)
                 o=1.0-th
                 p=o[0:8]
                 for b in range(1,KT//8): p=p*o[8*b:8*b+8]
@@ -464,7 +468,7 @@
         l8=lsum[:,0:128]
         for b in range(1,CH//128): l8+=lsum[:,128*b:128*(b+1)]
         loss_ref[0:8,:]+=l8*(1.0/negcount)
-        out=(hf*gh[:,width:width+1]-gh[:,:width])*rho
+        out=(hf*(1.0-jnp.sum(rs,1,keepdims=True))-gh[:,:width])*rho
         gh_ref[rows_of(kt),:width]=out.astype(bf16)
         live=kt+1<tiles
         na,ni=column(jnp.where(live,sp,1.0),jnp.where(live,nk,tiles))
@@ -486,7 +490,7 @@
                  pl.BlockSpec((1,width,ents),lambda j,c:(j,0,0)),
                  pl.BlockSpec((16,128),lambda j,c:(0,0))],
       scratch_shapes=[pltpu.VMEM((wa,ents),bf16),pltpu.VMEM((ents,wa),bf16),
-                      pltpu.VMEM((wa,ents),f32),pltpu.VMEM((8,ents),f32),pltpu.VMEM((KT,ents),f32)])
+                      pltpu.VMEM((wa,ents),f32),pltpu.VMEM((8,ents),f32),pltpu.VMEM((KT,ents),f32),pltpu.VMEM((8,ents),jnp.int32)])
     return pl.pallas_call(functools.partial(block_kernel,width,ents,negcount,CH),grid_spec=gs,name="k2_blocks",
       out_shape=[jax.ShapeDtypeStruct((h.shape[0],width),bf16),jax.ShapeDtypeStruct(tables.shape,f32),jax.ShapeDtypeStruct((16,128),f32)],
       compiler_params=pltpu.CompilerParams(vmem_limit_bytes=60<<20,dimension_semantics=("arbitrary",)))(counts,h,tables,dst,neg)
@@ -618,13 +622,13 @@
     rel(6)
     both(stZ,2)
     rel(7)
-    gload(0).wait()
     for i in range(nz): relpair(i).start()
     for i in range(last):
         relpair(i).wait_recv()
         rsz[i]=(racc[grp(2*order[i]+k),:]+rp[i]).astype(rsz.dtype)
         relz(i).start()
     both(stZ,3)
+    gload(0).wait()
     sq=jnp.zeros((RB,CK),f32)
     def gx(h,l): return rc(ge_ref.at[rows_of[h],l],ge_ref.at[rows_of[h],l],gxs.at[h],gxr.at[h],(xn,e))
     def gy(h,l): return rc(ge_ref.at[rows_of[h],l],ge_ref.at[rows_of[h],l],gys.at[h],gyr.at[h],(yn,e))
@@ -640,8 +644,6 @@
         if h==0: gx(0,lane(c)).start()
         else: gy(1,lane(c)).start()
     gy(0,lane(c)).start(); gx(1,lane(c)).start()
-    gx(0,lane(xn)).wait_recv(); gd(0,lane(xn)).start()
-    gy(1,lane(yn)).wait_recv(); gd(1,lane(yn)).start()
     relpair(last).wait_recv()
     rv=racc[grp(e),:]+rp[last]
     for i in range(last):
@@ -651,16 +653,26 @@
     one=jnp.sum(sq)+3.0*jnp.sum(rv*rv)
     row=lax.broadcasted_iota(i32,(8,128),0)
     v=jnp.where(row==0,one,jnp.where(row==1,jnp.sum(sc_ref[0:8,:]),jnp.where(row==2,jnp.sum(sc_ref[8:16,:]),0.0)))
-    for s,to in enumerate(((c,sib),(xn,e),(yn,e))):
+    def swap(s,v,to):
         scb[s]=v
         cp=rc(scb.at[s],scb.at[3+s],css.at[s],csr.at[s],to)
         cp.start(); cp.wait()
-        v=v+scb[3+s]
+        return v+scb[3+s]
+    v=swap(0,v,(c,sib))
     scb[6+z]=v
     def cz(d): return rc(scb.at[6+z],scb.at[6+z],czs.at[d],czr.at[d],(c,lax.rem(e+2*d,parts)))
     for d in range(1,nz): cz(d).start()
+    gx(0,lane(xn)).wait_recv(); gd(0,lane(xn)).start()
+    gy(1,lane(yn)).wait_recv(); gd(1,lane(yn)).start()
     for d in range(1,nz): cz(d).wait()
-    sco_ref[...]=(scb[6]+scb[7])+(scb[8]+scb[9])
+    v=(scb[6]+scb[7])+(scb[8]+scb[9])
+    v=swap(1,v,(xn,e))
+    v=swap(2,v,(yn,e))
+    live=v[2:3,:]
+    norm=jnp.sqrt(v[0:1,:])/live
+    clip=0.01/math.sqrt(4*parts*parts*cap)
+    scale=jnp.minimum(1.0,clip/norm)/live
+    sco_ref[...]=jnp.where(row==0,norm,jnp.where(row==3,scale,v))
     gx(1,lane(xn)).wait_recv(); gy(0,lane(yn)).wait_recv()
     gd(0,lane(3-c)).wait_recv(); gd(1,lane(3-c)).wait_recv()
     for h in range(2):
@@ -706,10 +718,9 @@
     neg_ids,
     bucket_counts,
 ):
-    parts, slots = src_ids.shape[2:]
+    parts = src_ids.shape[2]
     negcount = neg_ids.shape[3]
     nrel = rel_table.shape[1]
-    clip_level = 0.01 / math.sqrt(lax.axis_size("rel") * lax.axis_size("ent") * parts * slots)
     padded = -(-negcount // 1024) * 1024
     negs = jnp.pad(neg_ids[0, 0], ((0, 0), (0, padded - negcount)), constant_values=-1)
     tables, hidden, arrived = gather_call(
@@ -726,9 +737,7 @@
     ent_grad, rel_grad, totals = reduce_call(
         partial, back, src_ids[0, 0], rel_ids[0, 0], sums, nrel
     )
-    squares, loss_sum, total = totals[0, 0], totals[1, 0], totals[2, 0]
-    grad_norm = jnp.sqrt(squares) / total
-    scale = jnp.minimum(1.0, clip_level / grad_norm) / total
+    grad_norm, loss_sum, total, scale = totals[0, 0], totals[1, 0], totals[2, 0], totals[3, 0]
     new_ent, new_ent_m, new_ent_v = adamw(ent_table, entity_first_moment, ent_v, scale * ent_grad.T)
     new_rel, new_rel_m, new_rel_v = adamw(
         rel_table, relation_first_moment, rel_v, scale * rel_grad[None]

time: 319 us -> 323 us (1.013)
  Pallas kernels: 296 us -> 305 us
  between operations: 4.59 us -> 0.7 us
    pallas_call x1, Pallas kernels: 123 us -> 129 us  [reduce_call(): pl.pallas_call(reduce_kernel, name='k3_reduce', in_specs=[A, A, V, V, V],...]
where the time goes in v3:
time: 323 us; the launch traced here: 324 us
  Pallas kernels  305 us (94%)
  other arithmetic  13.7 us (4%)
  local copies, waits for them, and re-layouts  4.52 us (1%)
    pallas_call x1, Pallas kernels, reduce_call(): pl.pallas_call(reduce_kernel, name='k3_reduce', in_specs=[A, A, V, V, V],...  129 us
    pallas_call x1, Pallas kernels, run_blocks(): pl.pallas_call(functools.partial(block_kernel, width, ents, negcount, CH)...  90.9 us
    pallas_call x1, Pallas kernels, gather_call(): pl.pallas_call(gather_kernel, name='k1_gather', in_specs=[V] * 5, out_spe...  84.5 us
    convert_element_type x1, other arithmetic, cube_body(): new_ent.astype(jnp.bfloat16)  7.25 us

profile of v3, /device:TPU:8, one launch (start us, length us, event | category | flops | bytes accessed | tf_op | source)
XLA Modules:
  0.0 323.6 jit_solution(12656441957954206021)
XLA Ops:
  0.6 0.8 pad_bitcast_fusion
  1.4 0.6 copy.25
  2.0 1.4 copy.22.dst_ref
  3.5 84.5 %k1_gather.1 = (bf16[8,400,2048]{2,1,0:T(8,128)(2,1)}, bf16[10240,512]{1,0:T(8,128)(2,1)}, s32[8,8,128]{2,1,0:T(8,128)}) custom-call(f32[400,2048]{1,0:T(8,128)} %bitcast.23, f32[3,200,400]{2,1,0:T(8,128)} %rt_ref.1, s32[8,1280]{1,0:T(8,128)} %bitcast.24, s32[8,1280]{1,0:T(8,128)} %bitcast.26, s32[8,8,128]{2,1,0:T(8,128)} %bitcast.28), custom_call_target="tpu_custom_call" | custom-call | tf_op jit(solution)/shard_map/k1_gather/pallas_call | solution.py:350
  87.9 90.9 %k2_blocks.1 = (bf16[10240,400]{1,0:T(8,128)(2,1)}, f32[8,400,2048]{2,1,0:T(8,128)}, f32[16,128]{1,0:T(8,128)}) custom-call(s32[8]{0:T(128)} %bitcast.32, bf16[10240,512]{1,0:T(8,128)(2,1)} %get-tuple-element.20.h_ref, bf16[8,400,2048]{2,1,0:T(8,128)(2,1)} %get-tuple-element.21.t_ref, s32[8,5,256]{2,1,0:T(8,128)} %copy.22.dst_ref, s32[8,1,1024]{2,1,0:T(1,128)} %bitcast.30), custom_call_target="tpu_custom_call" | custom-call | tf_op jit(solution)/shard_map/k2_blocks/pallas_call | solution.py:494
  178.9 0.0 copy-start.1
  178.9 129.3 %k3_reduce.1 = (f32[400,2048]{1,0:T(8,128)}, f32[200,400]{1,0:T(8,128)}, f32[8,128]{1,0:T(8,128)}) custom-call(f32[8,400,2048]{2,1,0:T(8,128)} %get-tuple-element.23.g_ref, bf16[10240,400]{1,0:T(8,128)(2,1)} %get-tuple-element.24.gh_ref, s32[8,1280]{1,0:T(8,128)} %bitcast.25, s32[8,1280]{1,0:T(8,128)} %bitcast.27, f32[16,128]{1,0:T(8,128)} %get-tuple-element.25.sc_ref), custom_call_target="tpu_custom_call" | custom-call | tf_op jit(solution)/shard_map/k3_reduce/pallas_call | solution.py:695
  308.1 1.4 fusion.6
  309.5 0.0 copy-start.3
  309.5 2.0 multiply_multiply_fusion.1
  311.6 0.0 copy-done.1
  311.6 0.0 copy-start
  311.6 0.0 copy-start.2
  311.6 4.4 %fusion.2 = (bf16[3,200,400]{2,1,0:T(8,128)(2,1)}, f32[3,200,400]{2,1,0:T(8,128)}, f32[3,200,400]{2,1,0:T(8,128)}, f32[3,200,400]{2,1,0:T(8,128)}) fusion(f32[3,200,400]{2,1,0:T(8,128)S(1)} %copy-done.1, f32[200,400]{1,0:T(8,128)S(1)} %get-tuple-element.38, f32[3,200,400]{2,1,0:T(8,128)} %param.15, f32[200,400]{1,0:T(8,128)S(1)} %get-tuple-element.37, ...), kind=kLoop, calls=%fused_computation.12 | loop fusion | flops 3120000 | bytes 6880000 | tf_op jit(solution)/shard_map/convert_element_type | solution.py:756
  316.0 0.0 copy-done.3
  316.0 0.0 copy-done
  316.0 0.3 copy-done.2
  316.3 7.2 %fusion.3 = (bf16[2048,400]{0,1:T(8,128)(2,1)}, f32[2048,400]{0,1:T(8,128)}, f32[2048,400]{0,1:T(8,128)}, f32[2048,400]{0,1:T(8,128)}) fusion(f32[2048,400]{0,1:T(8,128)S(1)} %copy-done, f32[400,2048]{1,0:T(8,128)} %get-tuple-element.27, f32[]{:T(128)} %bitcast.10, f32[2048,400]{0,1:T(8,128)S(1)} %copy-done.2, f32[2048,400]{0,1:T(8,128)S(1)} %copy-done.3), kind=kLoop, calls=%fused_computation.13 | loop fusion | flops 13926400 | bytes 24576004 | tf_op jit(solution)/shard_map/convert_element_type | solution.py:752
Async XLA Ops:
  178.9 132.7 %copy-start.1 = (f32[3,200,400]{2,1,0:T(8,128)S(1)}, f32[3,200,400]{2,1,0:T(8,128)}, u32[]{:S(2)}) copy-start(f32[3,200,400]{2,1,0:T(8,128)} %rt_ref.1) | copy-start | bytes 2880004
  309.5 6.5 %copy-start.3 = (f32[2048,400]{0,1:T(8,128)S(1)}, f32[2048,400]{0,1:T(8,128)}, u32[]{:S(2)}) copy-start(f32[2048,400]{0,1:T(8,128)} %param.13) | copy-start | bytes 9830404
  311.6 4.5 %copy-start = (f32[2048,400]{0,1:T(8,128)S(1)}, f32[2048,400]{0,1:T(8,128)}, u32[]{:S(2)}) copy-start(f32[2048,400]{0,1:T(8,128)} %param.11) | copy-start | bytes 9830404
  311.6 4.8 %copy-start.2 = (f32[2048,400]{0,1:T(8,128)S(1)}, f32[2048,400]{0,1:T(8,128)}, u32[]{:S(2)}) copy-start(f32[2048,400]{0,1:T(8,128)} %param.12) | copy-start | bytes 9830404

commit v4 on v3

--- a/solution.py
+++ b/solution.py
@@ -357,9 +357,10 @@
 
 KT = 256
 WA=416
+SB=32
 def block_kernel(width, ents, negcount, CH,
                  counts_ref, h_ref, t_ref, dst_ref, neg_ref, gh_ref, g_ref, loss_ref,
-                 ta_ref, tr_ref, acc_ref, crow_ref, s_ref, lane_ref):
+                 ta_ref, tr_ref, acc_ref, crow_ref, s_ref, lane_ref, m_ref):
     j=pl.program_id(0)
     wa=ta_ref.shape[0]
     count=counts_ref[j]
@@ -394,12 +395,13 @@
     first=jnp.logical_and(lax.broadcasted_iota(jnp.int32,(8,128),0)==0,lax.broadcasted_iota(jnp.int32,(8,128),1)==0)
     loss_ref[8:16,:]+=jnp.where(first,count.astype(f32),0.0)
     eye=lax.broadcasted_iota(jnp.int32,(KT,KT),0)==lax.broadcasted_iota(jnp.int32,(KT,KT),1)
+    lanes=lax.broadcasted_iota(jnp.int32,(SB,CH),1).astype(f32).astype(bf16)
     lane_ref[...]=lax.broadcasted_iota(jnp.int32,lane_ref.shape,1)
     nch=ents//CH
     def rows_of(kt): return pl.ds(pl.multiple_of(kt*KT,KT),KT)
     def live_of(kt): return (lax.broadcasted_iota(jnp.int32,(KT,1),0)+kt*KT)<count
     def idcol(kt):
-        idr=dst_ref[0,pl.ds(kt,1),:].astype(f32)
+        idr=dst_ref[pl.ds(j,1),pl.ds(pl.multiple_of(kt*KT,KT),KT)].astype(f32)
         return jnp.sum(jnp.where(eye,idr,0.0),1,keepdims=True).astype(jnp.int32)
     def aug(kt):
         hb=h_ref[rows_of(kt),:]
@@ -441,34 +443,35 @@
         gh=jnp.zeros((KT,wa),f32)
         sp=jnp.zeros((KT,128),f32)
         lsum=jnp.zeros((8,CH),f32)
-        rs=jnp.zeros((KT,128),f32)
-        ms=[None]*nch
+        rs=[jnp.zeros((SB,128),f32)]*(KT//SB)
         invn=inva*(0.25/negcount)
         pend=None
         for ci in range(nch+1):
             if ci<nch:
                 cols=slice(ci*CH,(ci+1)*CH)
-                s=s_ref[:,cols]
-                r=lax.rsqrt(s)
-                th=jnp.tanh(margin*0.5-s*r)
+                cr=crow_ref[0:1,cols]
+                p=None
+                for sub in range(KT//SB):
+                    at=slice(sub*SB,(sub+1)*SB)
+                    s=s_ref[at,cols]
+                    r=lax.rsqrt(s)
+                    th=jnp.tanh(margin*0.5-s*r)
+                    mask=(idc[at]-ci*CH).astype(f32).astype(bf16)==lanes
+                    xf=((1.0+th)*cr)*(r*invn[at])
+                    for b in range(CH//128): rs[sub]=rs[sub]+xf[:,128*b:128*(b+1)]
+                    m_ref[at,cols]=jnp.where(mask,bf16(1.0),bf16(0.0))-xf.astype(bf16)
+                    o=1.0-th
+                    for b in range(SB//8): p=o[8*b:8*b+8] if p is None else p*o[8*b:8*b+8]
+                lsum+=(math.log(2.0)*(KT//8)-jnp.log(p))*cr
                 sp=post(sdot(ha,ci),nidc,ci,sp)
-                cr=crow_ref[0:1,cols]
-                mask=idc==lane_ref[0:1,cols]
-                xf=((1.0+th)*cr)*(r*invn)
-                for b in range(CH//128): rs=rs+xf[:,128*b:128*(b+1)]
-                ms[ci]=(jnp.where(mask,1.0,0.0)-xf).astype(bf16)
-                o=1.0-th
-                p=o[0:8]
-                for b in range(1,KT//8): p=p*o[8*b:8*b+8]
-                lsum+=(math.log(2.0)*(KT//8)-jnp.log(p))*cr
             if ci>=1:
                 pc=slice((ci-1)*CH,ci*CH)
-                gh+=jnp.dot(ms[ci-1],tr_ref[pc,:],preferred_element_type=f32)
-                acc_ref[:,pc]+=jnp.dot(hat,ms[ci-1],preferred_element_type=f32)
+                gh+=jnp.dot(m_ref[:,pc],tr_ref[pc,:],preferred_element_type=f32)
+                acc_ref[:,pc]+=jnp.dot(hat,m_ref[:,pc],preferred_element_type=f32)
         l8=lsum[:,0:128]
         for b in range(1,CH//128): l8+=lsum[:,128*b:128*(b+1)]
         loss_ref[0:8,:]+=l8*(1.0/negcount)
-        out=(hf*(1.0-jnp.sum(rs,1,keepdims=True))-gh[:,:width])*rho
+        out=(hf*(1.0-jnp.sum(jnp.concatenate(rs,0),1,keepdims=True))-gh[:,:width])*rho
         gh_ref[rows_of(kt),:width]=out.astype(bf16)
         live=kt+1<tiles
         na,ni=column(jnp.where(live,sp,1.0),jnp.where(live,nk,tiles))
@@ -484,13 +487,13 @@
     gs=pltpu.PrefetchScalarGridSpec(num_scalar_prefetch=1,grid=(parts,),
       in_specs=[pl.BlockSpec((cap,h.shape[1]),lambda j,c:(j,0)),
                 pl.BlockSpec((1,width,ents),lambda j,c:(j,0,0)),
-                pl.BlockSpec((1,cap//KT,KT),lambda j,c:(j,0,0)),
+                pl.BlockSpec((parts,cap),lambda j,c:(0,0)),
                 pl.BlockSpec((1,1,nn),lambda j,c:(j,0,0))],
       out_specs=[pl.BlockSpec((cap,width),lambda j,c:(j,0)),
                  pl.BlockSpec((1,width,ents),lambda j,c:(j,0,0)),
                  pl.BlockSpec((16,128),lambda j,c:(0,0))],
       scratch_shapes=[pltpu.VMEM((wa,ents),bf16),pltpu.VMEM((ents,wa),bf16),
-                      pltpu.VMEM((wa,ents),f32),pltpu.VMEM((8,ents),f32),pltpu.VMEM((KT,ents),f32),pltpu.VMEM((8,ents),jnp.int32)])
+                      pltpu.VMEM((wa,ents),f32),pltpu.VMEM((8,ents),f32),pltpu.VMEM((KT,ents),f32),pltpu.VMEM((8,ents),jnp.int32),pltpu.VMEM((KT,ents),bf16)])
     return pl.pallas_call(functools.partial(block_kernel,width,ents,negcount,CH),grid_spec=gs,name="k2_blocks",
       out_shape=[jax.ShapeDtypeStruct((h.shape[0],width),bf16),jax.ShapeDtypeStruct(tables.shape,f32),jax.ShapeDtypeStruct((16,128),f32)],
       compiler_params=pltpu.CompilerParams(vmem_limit_bytes=60<<20,dimension_semantics=("arbitrary",)))(counts,h,tables,dst,neg)
@@ -729,7 +732,7 @@
     back, partial, sums = run_blocks(
         hidden,
         tables,
-        dst_ids[0, 0].reshape(parts, -1, KT),
+        dst_ids[0, 0],
         arrived.reshape(parts, 1, padded),
         bucket_counts[0, 0],
         negcount,

time: 323 us -> 316 us (0.978)
  Pallas kernels: 305 us -> 297 us
    pallas_call x1, Pallas kernels: 90.9 us -> 78.6 us  [run_blocks(): pl.pallas_call(functools.partial(block_kernel, width, ents, negcount, CH)...]
    pallas_call x1, Pallas kernels: 129 us -> 134 us  [reduce_call(): pl.pallas_call(reduce_kernel, name='k3_reduce', in_specs=[A, A, V, V, V],...]
where the time goes in v4:
time: 316 us; the launch traced here: 315 us
  Pallas kernels  297 us (94%)
  other arithmetic  13.7 us (4%)
    pallas_call x1, Pallas kernels, reduce_call(): pl.pallas_call(reduce_kernel, name='k3_reduce', in_specs=[A, A, V, V, V],...  134 us
    pallas_call x1, Pallas kernels, gather_call(): pl.pallas_call(gather_kernel, name='k1_gather', in_specs=[V] * 5, out_spe...  84.5 us
    pallas_call x1, Pallas kernels, run_blocks(): pl.pallas_call(functools.partial(block_kernel, width, ents, negcount, CH)...  78.6 us
    convert_element_type x1, other arithmetic, cube_body(): new_ent.astype(jnp.bfloat16)  7.25 us

profile of v4, /device:TPU:8, one launch (start us, length us, event | category | flops | bytes accessed | tf_op | source)
XLA Modules:
  0.0 314.6 jit_solution(15424922366775013357)
XLA Ops:
  0.6 0.8 pad_bitcast_fusion
  1.4 0.6 copy.24
  2.0 84.5 %k1_gather.1 = (bf16[8,400,2048]{2,1,0:T(8,128)(2,1)}, bf16[10240,512]{1,0:T(8,128)(2,1)}, s32[8,8,128]{2,1,0:T(8,128)}) custom-call(f32[400,2048]{1,0:T(8,128)} %bitcast.23, f32[3,200,400]{2,1,0:T(8,128)} %rt_ref.1, s32[8,1280]{1,0:T(8,128)} %bitcast.24, s32[8,1280]{1,0:T(8,128)} %bitcast.26, s32[8,8,128]{2,1,0:T(8,128)} %bitcast.28), custom_call_target="tpu_custom_call" | custom-call | tf_op jit(solution)/shard_map/k1_gather/pallas_call | solution.py:350
  86.5 78.6 %k2_blocks.1 = (bf16[10240,400]{1,0:T(8,128)(2,1)}, f32[8,400,2048]{2,1,0:T(8,128)}, f32[16,128]{1,0:T(8,128)}) custom-call(s32[8]{0:T(128)} %bitcast.32, bf16[10240,512]{1,0:T(8,128)(2,1)} %get-tuple-element.20.h_ref, bf16[8,400,2048]{2,1,0:T(8,128)(2,1)} %get-tuple-element.21.t_ref, s32[8,1280]{1,0:T(8,128)} %bitcast.29, s32[8,1,1024]{2,1,0:T(1,128)} %bitcast.30), custom_call_target="tpu_custom_call" | custom-call | tf_op jit(solution)/shard_map/k2_blocks/pallas_call | solution.py:497
  165.1 0.0 copy-start.1
  165.1 134.0 %k3_reduce.1 = (f32[400,2048]{1,0:T(8,128)}, f32[200,400]{1,0:T(8,128)}, f32[8,128]{1,0:T(8,128)}) custom-call(f32[8,400,2048]{2,1,0:T(8,128)} %get-tuple-element.23.g_ref, bf16[10240,400]{1,0:T(8,128)(2,1)} %get-tuple-element.24.gh_ref, s32[8,1280]{1,0:T(8,128)} %bitcast.25, s32[8,1280]{1,0:T(8,128)} %bitcast.27, f32[16,128]{1,0:T(8,128)} %get-tuple-element.25.sc_ref), custom_call_target="tpu_custom_call" | custom-call | tf_op jit(solution)/shard_map/k3_reduce/pallas_call | solution.py:698
  299.2 1.4 fusion.6
  300.5 0.0 copy-start.3
  300.5 2.0 multiply_multiply_fusion.1
  302.6 0.0 copy-done.1
  302.6 0.0 copy-start
  302.6 0.0 copy-start.2
  302.6 4.4 %fusion.2 = (bf16[3,200,400]{2,1,0:T(8,128)(2,1)}, f32[3,200,400]{2,1,0:T(8,128)}, f32[3,200,400]{2,1,0:T(8,128)}, f32[3,200,400]{2,1,0:T(8,128)}) fusion(f32[3,200,400]{2,1,0:T(8,128)S(1)} %copy-done.1, f32[200,400]{1,0:T(8,128)S(1)} %get-tuple-element.38, f32[3,200,400]{2,1,0:T(8,128)} %param.15, f32[200,400]{1,0:T(8,128)S(1)} %get-tuple-element.37, ...), kind=kLoop, calls=%fused_computation.12 | loop fusion | flops 3120000 | bytes 6880000 | tf_op jit(solution)/shard_map/convert_element_type | solution.py:759
  307.1 0.0 copy-done.3
  307.1 0.0 copy-done
  307.1 0.3 copy-done.2
  307.4 7.2 %fusion.3 = (bf16[2048,400]{0,1:T(8,128)(2,1)}, f32[2048,400]{0,1:T(8,128)}, f32[2048,400]{0,1:T(8,128)}, f32[2048,400]{0,1:T(8,128)}) fusion(f32[2048,400]{0,1:T(8,128)S(1)} %copy-done, f32[400,2048]{1,0:T(8,128)} %get-tuple-element.27, f32[]{:T(128)} %bitcast.10, f32[2048,400]{0,1:T(8,128)S(1)} %copy-done.2, f32[2048,400]{0,1:T(8,128)S(1)} %copy-done.3), kind=kLoop, calls=%fused_computation.13 | loop fusion | flops 13926400 | bytes 24576004 | tf_op jit(solution)/shard_map/convert_element_type | solution.py:755
Async XLA Ops:
  165.1 137.5 %copy-start.1 = (f32[3,200,400]{2,1,0:T(8,128)S(1)}, f32[3,200,400]{2,1,0:T(8,128)}, u32[]{:S(2)}) copy-start(f32[3,200,400]{2,1,0:T(8,128)} %rt_ref.1) | copy-start | bytes 2880004
  300.5 6.5 %copy-start.3 = (f32[2048,400]{0,1:T(8,128)S(1)}, f32[2048,400]{0,1:T(8,128)}, u32[]{:S(2)}) copy-start(f32[2048,400]{0,1:T(8,128)} %param.13) | copy-start | bytes 9830404
  302.6 4.5 %copy-start = (f32[2048,400]{0,1:T(8,128)S(1)}, f32[2048,400]{0,1:T(8,128)}, u32[]{:S(2)}) copy-start(f32[2048,400]{0,1:T(8,128)} %param.11) | copy-start | bytes 9830404
  302.6 4.8 %copy-start.2 = (f32[2048,400]{0,1:T(8,128)S(1)}, f32[2048,400]{0,1:T(8,128)}, u32[]{:S(2)}) copy-start(f32[2048,400]{0,1:T(8,128)} %param.12) | copy-start | bytes 9830404

commit v5 on v4

--- a/solution.py
+++ b/solution.py
@@ -597,8 +597,8 @@
     def relpair(i): return rc(racc.at[grp(2*order[i]+1-k),:],rp.at[i],rps.at[i],rpr.at[i],(c,sib))
     def relz(i): return rc(rsz.at[i],rzr.at[i],rzs.at[i],rzrr.at[i],(c,2*order[i]+k))
     src(0)
+    both(st0,0)
     src(1)
-    both(st0,0)
     src(2)
     src(3)
     both(st0,1)
@@ -613,11 +613,11 @@
     both(stB,1)
     both(stZ,0)
     rel(0)
+    both(st0,3)
     rel(1)
-    both(st0,3)
-    rel(2)
     both(stB,2)
     both(stZ,1)
+    rel(2)
     rel(3)
     rel(4)
     rel(5)

time: 316 us -> 312 us (0.987)
    pallas_call x1, Pallas kernels: 134 us -> 114 us  [reduce_call(): pl.pallas_call(reduce_kernel, name='k3_reduce', in_specs=[A, A, V, V, V],...]
    pallas_call x1, Pallas kernels: 78.6 us -> 96 us  [run_blocks(): pl.pallas_call(functools.partial(block_kernel, width, ents, negcount, CH)...]
where the time goes in v5:
time: 312 us
  Pallas kernels  295 us (95%)
  other arithmetic  13.7 us (4%)
    pallas_call x1, Pallas kernels, reduce_call(): pl.pallas_call(reduce_kernel, name='k3_reduce', in_specs=[A, A, V, V, V],...  114 us
    pallas_call x1, Pallas kernels, run_blocks(): pl.pallas_call(functools.partial(block_kernel, width, ents, negcount, CH)...  96 us
    pallas_call x1, Pallas kernels, gather_call(): pl.pallas_call(gather_kernel, name='k1_gather', in_specs=[V] * 5, out_spe...  84.5 us
    convert_element_type x1, other arithmetic, cube_body(): new_ent.astype(jnp.bfloat16)  7.25 us

profile of v5, /device:TPU:8, one launch (start us, length us, event | category | flops | bytes accessed | tf_op | source)
XLA Modules:
  0.0 312.4 jit_solution(6471903568626175154)
XLA Ops:
  0.6 0.8 pad_bitcast_fusion
  1.4 0.6 copy.24
  2.0 84.5 %k1_gather.1 = (bf16[8,400,2048]{2,1,0:T(8,128)(2,1)}, bf16[10240,512]{1,0:T(8,128)(2,1)}, s32[8,8,128]{2,1,0:T(8,128)}) custom-call(f32[400,2048]{1,0:T(8,128)} %bitcast.23, f32[3,200,400]{2,1,0:T(8,128)} %rt_ref.1, s32[8,1280]{1,0:T(8,128)} %bitcast.24, s32[8,1280]{1,0:T(8,128)} %bitcast.26, s32[8,8,128]{2,1,0:T(8,128)} %bitcast.28), custom_call_target="tpu_custom_call" | custom-call | tf_op jit(solution)/shard_map/k1_gather/pallas_call | solution.py:350
  86.5 96.0 %k2_blocks.1 = (bf16[10240,400]{1,0:T(8,128)(2,1)}, f32[8,400,2048]{2,1,0:T(8,128)}, f32[16,128]{1,0:T(8,128)}) custom-call(s32[8]{0:T(128)} %bitcast.32, bf16[10240,512]{1,0:T(8,128)(2,1)} %get-tuple-element.20.h_ref, bf16[8,400,2048]{2,1,0:T(8,128)(2,1)} %get-tuple-element.21.t_ref, s32[8,1280]{1,0:T(8,128)} %bitcast.29, s32[8,1,1024]{2,1,0:T(1,128)} %bitcast.30), custom_call_target="tpu_custom_call" | custom-call | tf_op jit(solution)/shard_map/k2_blocks/pallas_call | solution.py:497
  182.5 0.0 copy-start.1
  182.5 114.5 %k3_reduce.1 = (f32[400,2048]{1,0:T(8,128)}, f32[200,400]{1,0:T(8,128)}, f32[8,128]{1,0:T(8,128)}) custom-call(f32[8,400,2048]{2,1,0:T(8,128)} %get-tuple-element.23.g_ref, bf16[10240,400]{1,0:T(8,128)(2,1)} %get-tuple-element.24.gh_ref, s32[8,1280]{1,0:T(8,128)} %bitcast.25, s32[8,1280]{1,0:T(8,128)} %bitcast.27, f32[16,128]{1,0:T(8,128)} %get-tuple-element.25.sc_ref), custom_call_target="tpu_custom_call" | custom-call | tf_op jit(solution)/shard_map/k3_reduce/pallas_call | solution.py:698
  297.0 1.4 fusion.6
  298.4 0.0 copy-start.3
  298.4 2.0 multiply_multiply_fusion.1
  300.4 0.0 copy-done.1
  300.4 0.0 copy-start
  300.4 0.0 copy-start.2
  300.4 4.4 %fusion.2 = (bf16[3,200,400]{2,1,0:T(8,128)(2,1)}, f32[3,200,400]{2,1,0:T(8,128)}, f32[3,200,400]{2,1,0:T(8,128)}, f32[3,200,400]{2,1,0:T(8,128)}) fusion(f32[3,200,400]{2,1,0:T(8,128)S(1)} %copy-done.1, f32[200,400]{1,0:T(8,128)S(1)} %get-tuple-element.38, f32[3,200,400]{2,1,0:T(8,128)} %param.15, f32[200,400]{1,0:T(8,128)S(1)} %get-tuple-element.37, ...), kind=kLoop, calls=%fused_computation.12 | loop fusion | flops 3120000 | bytes 6880000 | tf_op jit(solution)/shard_map/convert_element_type | solution.py:759
  304.9 0.0 copy-done.3
  304.9 0.0 copy-done
  304.9 0.3 copy-done.2
  305.2 7.2 %fusion.3 = (bf16[2048,400]{0,1:T(8,128)(2,1)}, f32[2048,400]{0,1:T(8,128)}, f32[2048,400]{0,1:T(8,128)}, f32[2048,400]{0,1:T(8,128)}) fusion(f32[2048,400]{0,1:T(8,128)S(1)} %copy-done, f32[400,2048]{1,0:T(8,128)} %get-tuple-element.27, f32[]{:T(128)} %bitcast.10, f32[2048,400]{0,1:T(8,128)S(1)} %copy-done.2, f32[2048,400]{0,1:T(8,128)S(1)} %copy-done.3), kind=kLoop, calls=%fused_computation.13 | loop fusion | flops 13926400 | bytes 24576004 | tf_op jit(solution)/shard_map/convert_element_type | solution.py:755
Async XLA Ops:
  182.5 117.9 %copy-start.1 = (f32[3,200,400]{2,1,0:T(8,128)S(1)}, f32[3,200,400]{2,1,0:T(8,128)}, u32[]{:S(2)}) copy-start(f32[3,200,400]{2,1,0:T(8,128)} %rt_ref.1) | copy-start | bytes 2880004
  298.4 6.5 %copy-start.3 = (f32[2048,400]{0,1:T(8,128)S(1)}, f32[2048,400]{0,1:T(8,128)}, u32[]{:S(2)}) copy-start(f32[2048,400]{0,1:T(8,128)} %param.13) | copy-start | bytes 9830404
  300.4 4.5 %copy-start = (f32[2048,400]{0,1:T(8,128)S(1)}, f32[2048,400]{0,1:T(8,128)}, u32[]{:S(2)}) copy-start(f32[2048,400]{0,1:T(8,128)} %param.11) | copy-start | bytes 9830404
  300.4 4.8 %copy-start.2 = (f32[2048,400]{0,1:T(8,128)S(1)}, f32[2048,400]{0,1:T(8,128)}, u32[]{:S(2)}) copy-start(f32[2048,400]{0,1:T(8,128)} %param.12) | copy-start | bytes 9830404

commit v6 on v4

--- a/solution.py
+++ b/solution.py
@@ -477,7 +477,7 @@
         na,ni=column(jnp.where(live,sp,1.0),jnp.where(live,nk,tiles))
         return na,ni,nidc
     lax.fori_loop(0,tiles,tile,(a0,i0,idc))
-    g_ref[0]=tf*acc_ref[width:width+1,:]+tf*acc_ref[width+1:width+2,:]+tf*acc_ref[width+2:width+3,:]-acc_ref[0:width,:]
+    g_ref[0]=tf*(acc_ref[width:width+1,:]+acc_ref[width+1:width+2,:]+acc_ref[width+2:width+3,:])-acc_ref[0:width,:]
 
 def run_blocks(h,tables,dst,neg,counts,negcount,CH=256):
     parts,width,ents=tables.shape

time: 316 us -> 311 us (0.984)
    pallas_call x1, Pallas kernels: 134 us -> 119 us  [reduce_call(): pl.pallas_call(reduce_kernel, name='k3_reduce', in_specs=[A, A, V, V, V],...]
    pallas_call x1, Pallas kernels: 78.6 us -> 90.7 us  [run_blocks(): pl.pallas_call(functools.partial(block_kernel, width, ents, negcount, CH)...]
where the time goes in v6:
time: 311 us; the launch traced here: 312 us
  Pallas kernels  294 us (95%)
  other arithmetic  13.7 us (4%)
    pallas_call x1, Pallas kernels, reduce_call(): pl.pallas_call(reduce_kernel, name='k3_reduce', in_specs=[A, A, V, V, V],...  119 us
    pallas_call x1, Pallas kernels, run_blocks(): pl.pallas_call(functools.partial(block_kernel, width, ents, negcount, CH)...  90.7 us
    pallas_call x1, Pallas kernels, gather_call(): pl.pallas_call(gather_kernel, name='k1_gather', in_specs=[V] * 5, out_spe...  84.5 us
    convert_element_type x1, other arithmetic, cube_body(): new_ent.astype(jnp.bfloat16)  7.25 us

profile of v6, /device:TPU:8, one launch (start us, length us, event | category | flops | bytes accessed | tf_op | source)
XLA Modules:
  0.0 311.5 jit_solution(17359490364263366129)
XLA Ops:
  0.6 0.8 pad_bitcast_fusion
  1.4 0.6 copy.24
  2.0 84.5 %k1_gather.1 = (bf16[8,400,2048]{2,1,0:T(8,128)(2,1)}, bf16[10240,512]{1,0:T(8,128)(2,1)}, s32[8,8,128]{2,1,0:T(8,128)}) custom-call(f32[400,2048]{1,0:T(8,128)} %bitcast.23, f32[3,200,400]{2,1,0:T(8,128)} %rt_ref.1, s32[8,1280]{1,0:T(8,128)} %bitcast.24, s32[8,1280]{1,0:T(8,128)} %bitcast.26, s32[8,8,128]{2,1,0:T(8,128)} %bitcast.28), custom_call_target="tpu_custom_call" | custom-call | tf_op jit(solution)/shard_map/k1_gather/pallas_call | solution.py:350
  86.5 90.7 %k2_blocks.1 = (bf16[10240,400]{1,0:T(8,128)(2,1)}, f32[8,400,2048]{2,1,0:T(8,128)}, f32[16,128]{1,0:T(8,128)}) custom-call(s32[8]{0:T(128)} %bitcast.32, bf16[10240,512]{1,0:T(8,128)(2,1)} %get-tuple-element.20.h_ref, bf16[8,400,2048]{2,1,0:T(8,128)(2,1)} %get-tuple-element.21.t_ref, s32[8,1280]{1,0:T(8,128)} %bitcast.29, s32[8,1,1024]{2,1,0:T(1,128)} %bitcast.30), custom_call_target="tpu_custom_call" | custom-call | tf_op jit(solution)/shard_map/k2_blocks/pallas_call | solution.py:497
  177.2 0.0 copy-start.1
  177.2 118.8 %k3_reduce.1 = (f32[400,2048]{1,0:T(8,128)}, f32[200,400]{1,0:T(8,128)}, f32[8,128]{1,0:T(8,128)}) custom-call(f32[8,400,2048]{2,1,0:T(8,128)} %get-tuple-element.23.g_ref, bf16[10240,400]{1,0:T(8,128)(2,1)} %get-tuple-element.24.gh_ref, s32[8,1280]{1,0:T(8,128)} %bitcast.25, s32[8,1280]{1,0:T(8,128)} %bitcast.27, f32[16,128]{1,0:T(8,128)} %get-tuple-element.25.sc_ref), custom_call_target="tpu_custom_call" | custom-call | tf_op jit(solution)/shard_map/k3_reduce/pallas_call | solution.py:698
  296.0 1.4 fusion.6
  297.4 0.0 copy-start.3
  297.4 2.0 multiply_multiply_fusion.1
  299.5 0.0 copy-done.1
  299.5 0.0 copy-start
  299.5 0.0 copy-start.2
  299.5 4.4 %fusion.2 = (bf16[3,200,400]{2,1,0:T(8,128)(2,1)}, f32[3,200,400]{2,1,0:T(8,128)}, f32[3,200,400]{2,1,0:T(8,128)}, f32[3,200,400]{2,1,0:T(8,128)}) fusion(f32[3,200,400]{2,1,0:T(8,128)S(1)} %copy-done.1, f32[200,400]{1,0:T(8,128)S(1)} %get-tuple-element.38, f32[3,200,400]{2,1,0:T(8,128)} %param.15, f32[200,400]{1,0:T(8,128)S(1)} %get-tuple-element.37, ...), kind=kLoop, calls=%fused_computation.12 | loop fusion | flops 3120000 | bytes 6880000 | tf_op jit(solution)/shard_map/convert_element_type | solution.py:759
  303.9 0.0 copy-done.3
  303.9 0.0 copy-done
  303.9 0.3 copy-done.2
  304.3 7.2 %fusion.3 = (bf16[2048,400]{0,1:T(8,128)(2,1)}, f32[2048,400]{0,1:T(8,128)}, f32[2048,400]{0,1:T(8,128)}, f32[2048,400]{0,1:T(8,128)}) fusion(f32[2048,400]{0,1:T(8,128)S(1)} %copy-done, f32[400,2048]{1,0:T(8,128)} %get-tuple-element.27, f32[]{:T(128)} %bitcast.10, f32[2048,400]{0,1:T(8,128)S(1)} %copy-done.2, f32[2048,400]{0,1:T(8,128)S(1)} %copy-done.3), kind=kLoop, calls=%fused_computation.13 | loop fusion | flops 13926400 | bytes 24576004 | tf_op jit(solution)/shard_map/convert_element_type | solution.py:755
Async XLA Ops:
  177.2 122.2 %copy-start.1 = (f32[3,200,400]{2,1,0:T(8,128)S(1)}, f32[3,200,400]{2,1,0:T(8,128)}, u32[]{:S(2)}) copy-start(f32[3,200,400]{2,1,0:T(8,128)} %rt_ref.1) | copy-start | bytes 2880004
  297.4 6.5 %copy-start.3 = (f32[2048,400]{0,1:T(8,128)S(1)}, f32[2048,400]{0,1:T(8,128)}, u32[]{:S(2)}) copy-start(f32[2048,400]{0,1:T(8,128)} %param.13) | copy-start | bytes 9830404
  299.5 4.5 %copy-start = (f32[2048,400]{0,1:T(8,128)S(1)}, f32[2048,400]{0,1:T(8,128)}, u32[]{:S(2)}) copy-start(f32[2048,400]{0,1:T(8,128)} %param.11) | copy-start | bytes 9830404
  299.5 4.8 %copy-start.2 = (f32[2048,400]{0,1:T(8,128)S(1)}, f32[2048,400]{0,1:T(8,128)}, u32[]{:S(2)}) copy-start(f32[2048,400]{0,1:T(8,128)} %param.12) | copy-start | bytes 9830404
